TPU v7x, 32 devices: a whole 2x2x4 slice. The times are simulated.
32 devices in a mesh: layer: 2 (over x), row: 4 (over y, core), col: 4 (over z).
Axes of the slice: x: 2, y: 2, z: 4, core: 2. Of those that a mesh axis runs over, the one named last changes fastest.
Arguments:
- density: bfloat16 [128, 12, 128, 128], P(('layer', 'row', 'col')), as said below
- pattern: int32 [128, 12], P(('layer', 'row', 'col')), may hold values from -1 to 127, as said below
- ham_derivative: bfloat16 [128, 12, 128, 128], P(('layer', 'row', 'col')), may hold values from -0.75 to 0.75
- pair_direction: bfloat16 [3, 128, 12, 1024], P(None, ('layer', 'row', 'col')), may hold values from -1 to 1
- atom_of_group: int32 [4096], P(('layer', 'row', 'col')), may hold values from 0 to 4095, each once
Outputs:
- next_density: bfloat16 [128, 12, 128, 128], P(('layer', 'row', 'col'))
- forces: float32 [3, 4096], P(None, ('layer', 'row', 'col'))
Inputs may be any that keep to these rules, and one draw needn't show every extreme that they name: `pattern`: row a lists distinct column blocks, each within 8 blocks of a counted around the 128 blocks in a loop, in rising order of that signed distance; a itself is always listed; unused slots hold -1 and come last; some row uses all 12 slots. `density`: zero in every slot where pattern is -1. `atom_of_group`: each atom is named once.
All inputs are finite; a program needn't handle non-finite values.
Results may differ from a plain program's by a relative error of at most 0.001.
Values may be sent and summed in bfloat16 or wider, within the bound.
No kernel may reach another device: no remote copies, remote signals or barrier semaphores. Data moves between devices by JAX's collectives and lax.ppermute only.
A program may use at most 192 MiB of HBM per device.

v0:
```python
import jax
import jax.numpy as jnp
from jax import lax
from jax.sharding import PartitionSpec as P


def shifted(block, axis, distance):
    devices = range(lax.axis_size(axis))
    route = [((i - distance) % len(devices), i) for i in devices]
    return lax.ppermute(block, axis, route)


def row_terms(left_blocks, wanted, through, turned, extended_pattern, derivative, direction):
    keep_count, block_size, _ = left_blocks.shape
    group_count = block_size // 4
    their_slots = extended_pattern[through]
    matches = (their_slots[:, None, :] == wanted[None, :, None]) & (wanted[None, :, None] >= 0)
    slot_index = jnp.sum(
        jnp.where(matches, jnp.arange(keep_count, dtype=jnp.int32)[None, None, :], 0), axis=2
    )
    present = jnp.any(matches, axis=2)
    slot_index = jnp.where(present, slot_index, keep_count)
    inner = jnp.arange(block_size, dtype=jnp.int32)
    right_blocks = turned[through[:, None, None], inner[None, :, None], slot_index[:, None, :]]
    right_wide = right_blocks.reshape(keep_count * block_size, keep_count * block_size)
    left_wide = jnp.transpose(left_blocks, (1, 0, 2)).reshape(block_size, keep_count * block_size)
    square = (
        jnp.dot(left_wide, right_wide, preferred_element_type=jnp.float32)
        .reshape(block_size, keep_count, block_size)
        .transpose(1, 0, 2)
    )
    mixture = 2.0 * left_blocks.astype(jnp.float32) - square
    energy = (
        (mixture * derivative.astype(jnp.float32))
        .reshape(keep_count, group_count, 4, group_count, 4)
        .sum(axis=(2, 4))
    )
    pair_factor = direction.astype(jnp.float32).reshape(3, keep_count, group_count, group_count)
    group_force = jnp.sum(pair_factor * energy[None], axis=(1, 3))
    return (mixture.astype(jnp.bfloat16), group_force)


def on_device(density, pattern, ham_derivative, pair_direction, atom_of_group):
    row_count = density.shape[0]
    group_count = density.shape[2] // 4
    blocks = row_count * lax.axis_size(("layer", "row", "col"))
    position = lax.axis_index(("layer", "row", "col"))
    received = {}
    for distance in (2, 1, -1, -2):
        received[distance] = shifted((density, pattern), ("layer", "row", "col"), distance)
    lower_far, lower_near, upper_near, upper_far = (
        received[2],
        received[1],
        received[-1],
        received[-2],
    )
    extended_density = jnp.concatenate(
        [lower_far[0], lower_near[0], density, upper_near[0], upper_far[0]], axis=0
    )
    extended_pattern = jnp.concatenate(
        [lower_far[1], lower_near[1], pattern, upper_near[1], upper_far[1]], axis=0
    )
    turned = jnp.transpose(extended_density, (0, 2, 1, 3))
    empty_slot = jnp.zeros((turned.shape[0], turned.shape[1], 1, turned.shape[3]), turned.dtype)
    turned = jnp.concatenate([turned, empty_slot], axis=2)
    anchor = position * row_count - 2 * row_count

    def visit(local_row):
        wanted = pattern[local_row]
        global_row = position * row_count + local_row
        through = jnp.mod(jnp.where(wanted >= 0, wanted, global_row) - anchor, blocks)
        return row_terms(
            density[local_row],
            wanted,
            through,
            turned,
            extended_pattern,
            ham_derivative[local_row],
            pair_direction[:, local_row],
        )

    next_density, group_force = lax.map(visit, jnp.arange(row_count, dtype=jnp.int32))
    flat = jnp.transpose(group_force, (1, 0, 2)).reshape(3, row_count * group_count)
    partial_value = jnp.zeros((3, blocks * group_count), jnp.float32).at[:, atom_of_group].set(flat)
    summed = lax.psum(partial_value, ("layer", "row", "col"))
    forces = lax.dynamic_slice_in_dim(
        summed, position * row_count * group_count, row_count * group_count, 1
    )
    return (next_density, forces)


def solution(mesh):
    placed = (
        P(("layer", "row", "col"), None, None, None),
        P(("layer", "row", "col"), None),
        P(("layer", "row", "col"), None, None, None),
        P(None, ("layer", "row", "col"), None, None),
        P(("layer", "row", "col")),
    )
    return jax.shard_map(
        on_device,
        mesh=mesh,
        in_specs=placed,
        out_specs=(P(("layer", "row", "col"), None, None, None), P(None, ("layer", "row", "col"))),
        check_vma=False,
    )
```

profile of v0, /device:TPU:0, one launch (start us, length us, event | category | flops | bytes accessed | tf_op | source)
XLA Modules:
  0.0 1907.4 jit_solution(3154570213275820604)
XLA Ops:
  14.2 194.9 %collective-permute-done = s32[4,12]{1,0:T(4,128)S(1)} collective-permute-done((s32[4,12]{1,0:T(4,128)}, s32[4,12]{1,0:T(4,128)S(1)}, u32[]{:S(2)}, u32[]{:S(2)}) %collective-permute-start) | collective-permute-done | bytes 224 | tf_op jit(solution)/shard_map/ppermute | solution.py:10
  209.1 6.8 collective-permute-done.1
  237.4 10.1 concatenate.17
  247.5 1574.9 %while.14 = (s32[]{:T(128)}, bf16[4,12,128,128]{3,2,1,0:T(8,128)(2,1)}, f32[4,3,32]{2,1,0:T(4,128)S(1)}, s32[4]{0:T(128)S(1)}, bf16[4,12,128,128]{3,2,1,0:T(8,12...) while((s32[]{:T(128)}, ...), condition=%wide.region_6.7_spmd, body=%wide.region_0.6_spmd.sunk | while | flops 605542144 | bytes 41671124 | solution.py:82
  253.0 355.1 %gather_fusion.1 = bf16[18432,128]{1,0:T(8,128)(2,1)} fusion(bf16[20,128,13,128]{3,1,2,0:T(8,128)(2,1)} %get-tuple-element.315, s32[18432]{0:T(1024)S(1)} %reshape.184), kind=kCustom, calls=%fused_computation.1.clone.1 | custom fusion | bytes 9658368 | tf_op jit(solution)/shard_map/while/body/eval_jaxpr/gather | solution.py:24
  608.2 9.8 reshape.185
  618.0 6.6 copy.40
  624.8 4.8 bitcast_dynamic-update-slice_fusion.4
  635.4 6.1 reduce_sum.52
  647.7 349.7 %gather_fusion.1 = bf16[18432,128]{1,0:T(8,128)(2,1)} fusion(bf16[20,128,13,128]{3,1,2,0:T(8,128)(2,1)} %get-tuple-element.315, s32[18432]{0:T(1024)S(1)} %reshape.184), kind=kCustom, calls=%fused_computation.1.clone.1 | custom fusion | bytes 9658368 | tf_op jit(solution)/shard_map/while/body/eval_jaxpr/gather | solution.py:24
  997.4 9.8 reshape.185
  1007.1 6.6 copy.40
  1014.0 4.8 bitcast_dynamic-update-slice_fusion.4
  1024.6 6.1 reduce_sum.52
  1036.8 357.7 %gather_fusion.1 = bf16[18432,128]{1,0:T(8,128)(2,1)} fusion(bf16[20,128,13,128]{3,1,2,0:T(8,128)(2,1)} %get-tuple-element.315, s32[18432]{0:T(1024)S(1)} %reshape.184), kind=kCustom, calls=%fused_computation.1.clone.1 | custom fusion | bytes 9658368 | tf_op jit(solution)/shard_map/while/body/eval_jaxpr/gather | solution.py:24
  1394.5 9.8 reshape.185
  1404.3 6.6 copy.40
  1411.2 4.8 bitcast_dynamic-update-slice_fusion.4
  1421.7 6.1 reduce_sum.52
  1434.0 354.5 %gather_fusion.1 = bf16[18432,128]{1,0:T(8,128)(2,1)} fusion(bf16[20,128,13,128]{3,1,2,0:T(8,128)(2,1)} %get-tuple-element.315, s32[18432]{0:T(1024)S(1)} %reshape.184), kind=kCustom, calls=%fused_computation.1.clone.1 | custom fusion | bytes 9658368 | tf_op jit(solution)/shard_map/while/body/eval_jaxpr/gather | solution.py:24
  1788.4 9.8 reshape.185
  1798.2 6.6 copy.40
  1815.7 6.1 reduce_sum.52
  1824.2 81.8 %psum.7 = f32[3,4096]{0,1:T(8,128)} all-reduce(f32[3,4096]{0,1:T(8,128)S(1)} %scatter_custom_fusion), channel_id=1, replica_groups=mesh['layer'=2,'row'=4,'col'=4] {'layer','row','col'}, use_global_device_ids=true, to_apply=%region_8.9 | all-reduce | flops 12288 | bytes 98304 | tf_op jit(solution)/shard_map/psum | solution.py:85
  (117 shorter events, 80.7 us)
Async XLA Ops:
  0.6 230.0 %copy-start = (bf16[4,12,128,128]{3,2,1,0:T(8,128)(2,1)S(1)}, bf16[4,12,128,128]{3,2,1,0:T(8,128)(2,1)}, u32[]{:S(2)}) copy-start(bf16[4,12,128,128]{3,2,1,0:T(8,128)(2,1)} %param.7) | copy-start | bytes 4718596
  0.6 224.5 %collective-permute-start.4 = (bf16[4,12,128,128]{3,2,1,0:T(8,128)(2,1)}, bf16[4,12,128,128]{3,2,1,0:T(8,128)(2,1)}, u32[]{:S(2)}, u32[]{:S(2)}) collective-permute-start(bf16[4,12,128,128]{3,2,1,0:T(8,128)(2,1)} %param.7), channel_id=1, source_target_pairs={{30,0},{31,1},{0,2},{1,3},{2,4},{3,5},{4,6},{5,7},{6,8},{7,9},{8,1... | collective-permute-start | bytes 4718600 | tf_op jit(solution)/shard_map/ppermute | solution.py:10
  4.7 223.2 %collective-permute-start.5 = (bf16[4,12,128,128]{3,2,1,0:T(8,128)(2,1)}, bf16[4,12,128,128]{3,2,1,0:T(8,128)(2,1)}, u32[]{:S(2)}, u32[]{:S(2)}) collective-permute-start(bf16[4,12,128,128]{3,2,1,0:T(8,128)(2,1)} %param.7), channel_id=1, source_target_pairs={{31,0},{0,1},{1,2},{2,3},{3,4},{4,5},{5,6},{6,7},{7,8},{8,9},{9,10... | collective-permute-start | bytes 4718600 | tf_op jit(solution)/shard_map/ppermute | solution.py:10
  6.3 225.6 %collective-permute-start.6 = (bf16[4,12,128,128]{3,2,1,0:T(8,128)(2,1)}, bf16[4,12,128,128]{3,2,1,0:T(8,128)(2,1)}, u32[]{:S(2)}, u32[]{:S(2)}) collective-permute-start(bf16[4,12,128,128]{3,2,1,0:T(8,128)(2,1)} %param.7), channel_id=1, source_target_pairs={{1,0},{2,1},{3,2},{4,3},{5,4},{6,5},{7,6},{8,7},{9,8},{10,9},{11,1... | collective-permute-start | bytes 4718600 | tf_op jit(solution)/shard_map/ppermute | solution.py:10
  10.1 224.6 %collective-permute-start.7 = (bf16[4,12,128,128]{3,2,1,0:T(8,128)(2,1)}, bf16[4,12,128,128]{3,2,1,0:T(8,128)(2,1)}, u32[]{:S(2)}, u32[]{:S(2)}) collective-permute-start(bf16[4,12,128,128]{3,2,1,0:T(8,128)(2,1)} %param.7), channel_id=1, source_target_pairs={{2,0},{3,1},{4,2},{5,3},{6,4},{7,5},{8,6},{9,7},{10,8},{11,9},{12,... | collective-permute-start | bytes 4718600 | tf_op jit(solution)/shard_map/ppermute | solution.py:10
  10.1 199.0 %collective-permute-start = (s32[4,12]{1,0:T(4,128)}, s32[4,12]{1,0:T(4,128)S(1)}, u32[]{:S(2)}, u32[]{:S(2)}) collective-permute-start(s32[4,12]{1,0:T(4,128)} %param.8), channel_id=1, source_target_pairs={{30,0},{31,1},{0,2},{1,3},{2,4},{3,5},{4,6},{5,7},{6,8},{7,9},{8,1... | collective-permute-start | bytes 584 | tf_op jit(solution)/shard_map/ppermute | solution.py:10
  209.1 6.8 collective-permute-start.1
  215.9 3.8 collective-permute-start.2
  219.7 4.7 collective-permute-start.3
  237.4 10.1 copy-start.1
  237.4 10.1 copy-start.2
where the time goes:
time: 1920 us; the launch traced here: 1910 us
  local copies, waits for them, and re-layouts  1540 us (80%)
  waiting for transfers between devices  210 us (11%)
  blocking collectives  81.8 us (4%)
  other arithmetic  35 us (2%)
    gather x4, local copies, waits for them, and re-layouts, row_terms(): turned[through[:, None, None], inner[None, :, None], slot_index[:, None, :]]  1420 us
    ppermute x8, waiting for transfers between devices, shifted(): return lax.ppermute(block, axis, route)  210 us
    psum x1, blocking collectives, on_device(): summed = lax.psum(partial_value, ('layer', 'row', 'col'))  81.8 us
    reshape x4, local copies, waits for them, and re-layouts, row_terms(): right_blocks.reshape(keep_count * block_size, keep_count * block_size)  39.2 us
  transfers between devices with their start and end apart: 8, of which 4 were waited for; matrix products, arithmetic and copies ran while one was open for 1% of the time, Pallas kernels for 0%

commit v1 on v0

v1 whole, which is shorter than its diff:
```python
import functools

import jax
import jax.numpy as jnp
from jax import lax
from jax.experimental import pallas as pl
from jax.experimental.pallas import tpu as pltpu
from jax.sharding import PartitionSpec as P

AXES = ("layer", "row", "col")


def hop(value, distance, keep):
    total = lax.axis_size(AXES)
    line = lax.axis_size("col")
    route = [((i - distance) % total, i) for i in range(total) if keep(i % line)]
    return lax.ppermute(value, AXES, route)


def gathered(block, line):
    up1 = hop(block, 1, lambda z: z >= 1)
    down1 = hop(block, -1, lambda z: z <= line - 2)
    up2 = hop(up1, 1, lambda z: z >= 2)
    down2 = hop(down1, -1, lambda z: z <= line - 3)
    up = {1: up1, 2: up2}
    down = {1: down1, 2: down2}
    for step in range(3, line):
        up[step] = hop(up[step - 1], 1, lambda z, step=step: z >= step)
        down[step] = hop(down[step - 1], -1, lambda z, step=step: z <= line - 1 - step)
    over_far = hop(up[line - 2], -line, lambda z: z >= line - 2)
    over_near = hop(up[line - 1], -line, lambda z: z == line - 1)
    under_far = hop(down[line - 2], line, lambda z: z <= 1)
    under_near = hop(down[line - 1], line, lambda z: z == 0)
    return up1, up2, down1, down2, under_near, under_far, over_near, over_far


def step_kernel(
    rows, keep, where_ref, column_ref, place_ref,
    own, up1, up2, down1, down2, under_near, under_far, over_near, over_far,
    ham_ref, factor_ref,
    next_ref, force_ref,
    held, left, square, product, sems,
):
    size = own.shape[2]
    groups = size // 4
    span = 5 * rows
    batch = rows * keep
    z = place_ref[0]
    line = place_ref[1]

    def fetch(part, near, far, condition):
        spot = held.at[pl.ds(part * batch, batch)]

        @pl.when(condition)
        def _():
            pltpu.make_async_copy(near, spot, sems.at[part]).start()

        if far is not None:

            @pl.when(jnp.logical_not(condition))
            def _():
                pltpu.make_async_copy(far, spot, sems.at[part]).start()

    fetch(2, own, None, z >= 0)
    fetch(1, up1, under_near, z >= 1)
    fetch(3, down1, over_near, z <= line - 2)
    fetch(0, up2, under_far, z >= 2)
    fetch(4, down2, over_far, z <= line - 3)

    held[span * keep] = jnp.zeros((size, size), held.dtype)
    left[...] = jnp.zeros(left.shape, left.dtype)

    def arrived(part):
        spot = held.at[pl.ds(part * batch, batch)]
        pltpu.make_async_copy(own, spot, sems.at[part]).wait()

    arrived(2)
    for i in range(rows):
        for l in range(keep):
            column = column_ref[i, l]

            @pl.when(column >= 0)
            def _(i=i, l=l, column=column):
                at = pl.multiple_of(column * size, size)
                left[i * size : (i + 1) * size, pl.ds(at, size)] = held[2 * batch + i * keep + l]

    for part in (1, 3, 0, 4):
        arrived(part)

    reach = 2 * rows
    for j in range(0, span, 2):
        low, high = max(0, j - reach), min(span, j + 2 + reach)
        right = jnp.concatenate(
            [
                jnp.concatenate([held[where_ref[r, j]], held[where_ref[r, j + 1]]], axis=1)
                for r in range(low, high)
            ],
            axis=0,
        )
        total = jnp.dot(left[:, low * size : high * size], right, preferred_element_type=jnp.float32)
        square[j] = total[:, :size]
        square[j + 1] = total[:, size:]

    for i in range(rows):

        def slot(k, sums, i=i):
            column = column_ref[i, k]
            term = square[jnp.maximum(column, 0), i * size : (i + 1) * size, :]
            term = jnp.where(column >= 0, term, 0.0)
            block = held[2 * batch + i * keep + k].astype(jnp.float32)
            mixture = 2.0 * block - term
            next_ref[i, k] = mixture.astype(next_ref.dtype)
            product[...] = mixture * ham_ref[i, k].astype(jnp.float32)
            energy = product[pl.ds(0, groups, stride=4), :]
            for r in range(1, 4):
                energy = energy + product[pl.ds(r, groups, stride=4), :]
            return tuple(sums[d] + energy * factor_ref[d, i, k].astype(jnp.float32) for d in range(3))

        start = tuple(jnp.zeros((groups, size), jnp.float32) for _ in range(3))
        sums = lax.fori_loop(0, keep, slot, start)
        for d in range(3):
            force_ref[d, i] = sums[d]


def on_device(density, pattern, ham_derivative, pair_direction, atom_of_group):
    rows, keep, size, _ = density.shape
    groups = size // 4
    devices = lax.axis_size(AXES)
    line = lax.axis_size("col")
    blocks = rows * devices
    atoms = blocks * groups
    position = lax.axis_index(AXES)

    patterns = {d: hop(pattern, d, lambda z: True) for d in (2, 1, -1, -2)}
    extended = jnp.concatenate([patterns[2], patterns[1], pattern, patterns[-1], patterns[-2]], axis=0)
    anchor = position * rows - 2 * rows
    span = 5 * rows
    relative = jnp.where(extended >= 0, jnp.mod(extended - anchor, blocks), -1)
    flat_slot = jnp.arange(span * keep, dtype=jnp.int32).reshape(span, keep, 1)
    hit = relative[:, :, None] == jnp.arange(span, dtype=jnp.int32)[None, None, :]
    where = jnp.min(jnp.where(hit, flat_slot, span * keep), axis=1)
    columns = relative[2 * rows : 3 * rows]
    place = jnp.stack([lax.axis_index("col"), jnp.int32(line)]).astype(jnp.int32)

    spread = jnp.repeat(jnp.eye(groups, dtype=jnp.bfloat16), 4, axis=1)
    factor = jnp.dot(pair_direction.reshape(3 * rows * keep * groups, groups), spread)
    factor = factor.reshape(3, rows, keep, groups, size)
    mine = (atom_of_group[:, None] == jnp.arange(atoms, dtype=jnp.int32)[None, :]).astype(jnp.float32)

    near = gathered(density, line)

    any_space = pl.BlockSpec(memory_space=pl.ANY)
    vmem = pl.BlockSpec(memory_space=pltpu.VMEM)
    smem = pl.BlockSpec(memory_space=pltpu.SMEM)
    next_density, sums = pl.pallas_call(
        functools.partial(step_kernel, rows, keep),
        out_shape=(
            jax.ShapeDtypeStruct(density.shape, density.dtype),
            jax.ShapeDtypeStruct((3, rows, groups, size), jnp.float32),
        ),
        in_specs=[smem] * 3 + [any_space] * 9 + [vmem] * 2,
        out_specs=(vmem, vmem),
        scratch_shapes=[
            pltpu.VMEM((span * keep + 1, size, size), jnp.bfloat16),
            pltpu.VMEM((rows * size, span * size), jnp.bfloat16),
            pltpu.VMEM((span, rows * size, size), jnp.float32),
            pltpu.VMEM((size, size), jnp.float32),
            pltpu.SemaphoreType.DMA((5,)),
        ],
        compiler_params=pltpu.CompilerParams(vmem_limit_bytes=48 * 1024 * 1024),
    )(
        where,
        columns,
        place,
        *[x.reshape(rows * keep, size, size) for x in (density, *near)],
        ham_derivative,
        factor,
    )
    flat = jnp.sum(sums, axis=3).reshape(3, rows * groups)
    spread_out = jnp.dot(flat, mine, precision=lax.Precision.HIGHEST)
    pieces = lax.all_to_all(
        spread_out.reshape(3, devices, rows * groups), AXES, split_axis=1, concat_axis=1, tiled=True
    )
    return next_density, jnp.sum(pieces, axis=1)


def solution(mesh):
    spread = P(AXES, None, None, None)
    return jax.shard_map(
        on_device,
        mesh=mesh,
        in_specs=(spread, P(AXES, None), spread, P(None, AXES, None, None), P(AXES)),
        out_specs=(spread, P(None, AXES)),
        check_vma=False,
    )
```

time: 1920 us -> 167 us (0.09)
  local copies, waits for them, and re-layouts: 1540 us -> 6.53 us
  waiting for transfers between devices: 210 us -> 109 us
  blocking collectives: 81.8 us -> 11.7 us
  other arithmetic: 35 us -> 1 us
    gather x8 -> x0, local copies, waits for them, and re-layouts: 1420 us -> none  [the longest x4 1420 us: row_terms(): turned[through[:, None, None], inner[None, :, None], slot_index[:, None, :]]]
    ppermute x8 -> x14, waiting for transfers between devices: 210 us -> 109 us  [hop(): return lax.ppermute(value, AXES, route)]
    psum x1 -> x0, blocking collectives: 81.8 us -> none  [on_device(): summed = lax.psum(partial_value, ('layer', 'row', 'col'))]
    reshape x6 -> x2, local copies, waits for them, and re-layouts: 39.4 us -> 0.98 us  [the longest x1 0.9 us: on_device(): pair_direction.reshape(3 * rows * keep * groups, groups)]
    reduce_sum x16 -> x2, other arithmetic: 27.3 us -> 0.75 us  [the longest x1 0.62 us: on_device(): return (next_density, jnp.sum(pieces, axis=1))]
    dot_general x4 -> x1, local copies, waits for them, and re-layouts: 26.4 us -> 1.76 us  [on_device(): jnp.dot(pair_direction.reshape(3 * rows * keep * groups, groups), spread)]
    mul x8 -> x0, local copies, waits for them, and re-layouts: 19.5 us -> none  [the longest x4 18.8 us: row_terms(): mixture * derivative.astype(jnp.float32)]
  transfers between devices with their start and end apart: 8 -> 14, of which waited for: 4 -> 7; matrix products, arithmetic and copies ran while one was open for 1% -> 3% of each run, Pallas kernels for 0% -> 0%
where the time goes in v1:
time: 167 us
  waiting for transfers between devices  109 us (65%)
  starting transfers between devices  22.9 us (14%)
  Pallas kernels  11.9 us (7%)
  blocking collectives  11.7 us (7%)
  local copies, waits for them, and re-layouts  6.53 us (4%)
  matrix products  2.95 us (2%)
    ppermute x14, waiting for transfers between devices, hop(): return lax.ppermute(value, AXES, route)  109 us
    ppermute x14, starting transfers between devices, hop(): return lax.ppermute(value, AXES, route)  22.9 us
    pallas_call x1, Pallas kernels, on_device(): pl.pallas_call(functools.partial(step_kernel, rows, keep), out_shape=(jax...  11.9 us
    all_to_all x1, blocking collectives, on_device(): lax.all_to_all(spread_out.reshape(3, devices, rows * groups), AXES, split...  11.7 us
    unnamed x13, local copies, waits for them, and re-layouts  3.62 us
  transfers between devices with their start and end apart: 14, of which 7 were waited for; matrix products, arithmetic and copies ran while one was open for 3% of the time, Pallas kernels for 0%

profile of v1, /device:TPU:0, one launch (start us, length us, event | category | flops | bytes accessed | tf_op | source)
XLA Modules:
  0.0 166.9 jit_solution(10483870814853372512)
XLA Ops:
  0.6 1.3 collective-permute-start.6
  1.9 5.7 %collective-permute-start.4 = (bf16[4,12,128,128]{3,2,1,0:T(8,128)(2,1)}, bf16[4,12,128,128]{3,2,1,0:T(8,128)(2,1)S(1)}, u32[]{:S(2)}, u32[]{:S(2)}) collective-permute-start(bf16[4,12,128,128]{3,2,1,0:T(8,128)(2,1)} %param.5), channel_id=1, source_target_pairs={{0,1},{1,2},{2,3},{4,5},{5,6},{6,7},{8,9},{9,10},{10,11},{12,13},{... | collective-permute-start | bytes 4718600 | tf_op jit(solution)/shard_map/ppermute | solution.py:17
  7.6 32.6 %collective-permute-done.6 = bf16[4,12,128,128]{3,2,1,0:T(8,128)(2,1)S(1)} collective-permute-done((bf16[4,12,128,128]{3,2,1,0:T(8,128)(2,1)}, bf16[4,12,128,128]{3,2,1,0:T(8,128)(2,1)S(1)}, u32[]{:S(2)}, u32[]{:S(2)}) %collective-permute-start.6) | collective-permute-done | bytes 1572896 | tf_op jit(solution)/shard_map/ppermute | solution.py:17
  40.2 1.3 collective-permute-start.7
  41.5 1.8 %collective-permute-start.5 = (bf16[4,12,128,128]{3,2,1,0:T(8,128)(2,1)S(1)}, bf16[4,12,128,128]{3,2,1,0:T(8,128)(2,1)}, u32[]{:S(2)}, u32[]{:S(2)}) collective-permute-start(bf16[4,12,128,128]{3,2,1,0:T(8,128)(2,1)S(1)} %collective-permute-done.4), channel_id=1, source_target_pairs={{1,2},{2,3},{5,6},{6,7},{9,10},{10,11},{13,14},{14,15},{17,18},{18... | collective-permute-start | bytes 4718600 | tf_op jit(solution)/shard_map/ppermute | solution.py:17
  44.4 33.3 %collective-permute-done.7 = bf16[4,12,128,128]{3,2,1,0:T(8,128)(2,1)} collective-permute-done((bf16[4,12,128,128]{3,2,1,0:T(8,128)(2,1)S(1)}, bf16[4,12,128,128]{3,2,1,0:T(8,128)(2,1)}, u32[]{:S(2)}, u32[]{:S(2)}) %collective-permute-start.7) | collective-permute-done | bytes 1572896 | tf_op jit(solution)/shard_map/ppermute | solution.py:17
  77.7 1.3 collective-permute-start.8
  79.0 1.8 %collective-permute-start.11 = (bf16[4,12,128,128]{3,2,1,0:T(8,128)(2,1)}, bf16[4,12,128,128]{3,2,1,0:T(8,128)(2,1)}, u32[]{:S(2)}, u32[]{:S(2)}) collective-permute-start(bf16[4,12,128,128]{3,2,1,0:T(8,128)(2,1)} %collective-permute-done.5), channel_id=1, source_target_pairs={{2,3},{6,7},{10,11},{14,15},{18,19},{22,23},{26,27},{30,31}} | collective-permute-start | bytes 4718600 | tf_op jit(solution)/shard_map/ppermute | solution.py:17
  80.9 1.9 %collective-permute-start.10 = (bf16[4,12,128,128]{3,2,1,0:T(8,128)(2,1)}, bf16[4,12,128,128]{3,2,1,0:T(8,128)(2,1)}, u32[]{:S(2)}, u32[]{:S(2)}) collective-permute-start(bf16[4,12,128,128]{3,2,1,0:T(8,128)(2,1)} %collective-permute-done.7), channel_id=1, source_target_pairs={{28,0},{29,1},{0,4},{1,5},{4,8},{5,9},{8,12},{9,13},{12,16},{13,17... | collective-permute-start | bytes 4718600 | tf_op jit(solution)/shard_map/ppermute | solution.py:17
  82.8 1.8 %collective-permute-start.13 = (bf16[4,12,128,128]{3,2,1,0:T(8,128)(2,1)}, bf16[4,12,128,128]{3,2,1,0:T(8,128)(2,1)}, u32[]{:S(2)}, u32[]{:S(2)}) collective-permute-start(bf16[4,12,128,128]{3,2,1,0:T(8,128)(2,1)} %collective-permute-done.5), channel_id=1, source_target_pairs={{6,2},{7,3},{10,6},{11,7},{14,10},{15,11},{18,14},{19,15},{22,18},... | collective-permute-start | bytes 4718600 | tf_op jit(solution)/shard_map/ppermute | solution.py:17
  84.6 30.0 %collective-permute-done.8 = bf16[4,12,128,128]{3,2,1,0:T(8,128)(2,1)} collective-permute-done((bf16[4,12,128,128]{3,2,1,0:T(8,128)(2,1)}, bf16[4,12,128,128]{3,2,1,0:T(8,128)(2,1)}, u32[]{:S(2)}, u32[]{:S(2)}) %collective-permute-start.8) | collective-permute-done | bytes 1572896 | tf_op jit(solution)/shard_map/ppermute | solution.py:17
  114.6 1.9 %collective-permute-start.9 = (bf16[4,12,128,128]{3,2,1,0:T(8,128)(2,1)}, bf16[4,12,128,128]{3,2,1,0:T(8,128)(2,1)}, u32[]{:S(2)}, u32[]{:S(2)}) collective-permute-start(bf16[4,12,128,128]{3,2,1,0:T(8,128)(2,1)} %collective-permute-done.8), channel_id=1, source_target_pairs={{28,0},{0,4},{4,8},{8,12},{12,16},{16,20},{20,24},{24,28}} | collective-permute-start | bytes 4718600 | tf_op jit(solution)/shard_map/ppermute | solution.py:17
  116.5 1.9 %collective-permute-start.12 = (bf16[4,12,128,128]{3,2,1,0:T(8,128)(2,1)}, bf16[4,12,128,128]{3,2,1,0:T(8,128)(2,1)}, u32[]{:S(2)}, u32[]{:S(2)}) collective-permute-start(bf16[4,12,128,128]{3,2,1,0:T(8,128)(2,1)} %collective-permute-done.11), channel_id=1, source_target_pairs={{7,3},{11,7},{15,11},{19,15},{23,19},{27,23},{31,27},{3,31}} | collective-permute-start | bytes 4718600 | tf_op jit(solution)/shard_map/ppermute | solution.py:17
  121.5 1.5 convolution_bitcast_fusion
  123.0 1.5 collective-permute-done
  124.5 1.2 collective-permute-start.1
  125.6 5.5 %collective-permute-done.1 = s32[4,12]{1,0:T(4,128)S(1)} collective-permute-done((s32[4,12]{1,0:T(4,128)S(1)}, s32[4,12]{1,0:T(4,128)S(1)}, u32[]{:S(2)}, u32[]{:S(2)}) %collective-permute-start.1) | collective-permute-done | bytes 224 | tf_op jit(solution)/shard_map/ppermute | solution.py:17
  131.2 3.6 %collective-permute-done.2 = s32[4,12]{1,0:T(4,128)S(1)} collective-permute-done((s32[4,12]{1,0:T(4,128)S(1)}, s32[4,12]{1,0:T(4,128)S(1)}, u32[]{:S(2)}, u32[]{:S(2)}) %collective-permute-start.2) | collective-permute-done | bytes 224 | tf_op jit(solution)/shard_map/ppermute | solution.py:17
  134.8 1.8 %copy.12 = bf16[4608,128]{1,0:T(8,128)(2,1)S(1)} copy(bf16[4608,128]{0,1:T(8,128)(2,1)} %convolution_bitcast_fusion) | data formatting | bytes 2359296 | tf_op jit(solution)/shard_map/dot_general | solution.py:146
  136.5 2.7 %collective-permute-done.3 = s32[4,12]{1,0:T(4,128)S(1)} collective-permute-done((s32[4,12]{1,0:T(4,128)S(1)}, s32[4,12]{1,0:T(4,128)S(1)}, u32[]{:S(2)}, u32[]{:S(2)}) %collective-permute-start.3) | collective-permute-done | bytes 224 | tf_op jit(solution)/shard_map/ppermute | solution.py:17
  139.6 1.4 copy-done.2
  141.0 11.9 %shard_map.68 = (bf16[4,12,128,128]{3,2,1,0:T(8,128)(2,1)}, f32[3,4,32,128]{3,2,1,0:T(8,128)S(1)}) custom-call(s32[20,20]{1,0:T(8,128)S(1)} %select_reduce_fusion.where_ref, s32[4,12]{1,0:T(4,128)S(1)} %slice.4.column_ref, s32[2]{0:T(128)S(1)} %pad_add_fusion.place_ref, bf16[48,128,128]{2,1,0:T(8,128)(2,1)S(1)} %bitcast.18, ...), custom_call_target="tpu_custom_call" | custom-call | tf_op jit(solution)/shard_map/pallas_call | solution.py:155
  153.1 1.5 fusion
  154.6 11.7 %all_to_all.5 = f32[3,32,128]{2,0,1:T(4,128)S(1)} all-to-all(f32[3,32,128]{2,0,1:T(4,128)S(1)} %fusion), channel_id=1, replica_groups=mesh['layer'=2,'row'=4,'col'=4] {'layer','row','col'}, dimensions={1} | all-to-all | bytes 98304 | tf_op jit(solution)/shard_map/all_to_all | solution.py:181
  (36 shorter events, 5.3 us)
Async XLA Ops:
  0.6 39.5 %collective-permute-start.6 = (bf16[4,12,128,128]{3,2,1,0:T(8,128)(2,1)}, bf16[4,12,128,128]{3,2,1,0:T(8,128)(2,1)S(1)}, u32[]{:S(2)}, u32[]{:S(2)}) collective-permute-start(bf16[4,12,128,128]{3,2,1,0:T(8,128)(2,1)} %param.5), channel_id=1, source_target_pairs={{1,0},{2,1},{3,2},{5,4},{6,5},{7,6},{9,8},{10,9},{11,10},{13,12},{... | collective-permute-start | bytes 4718600 | tf_op jit(solution)/shard_map/ppermute | solution.py:17
  1.9 39.5 %collective-permute-start.4 = (bf16[4,12,128,128]{3,2,1,0:T(8,128)(2,1)}, bf16[4,12,128,128]{3,2,1,0:T(8,128)(2,1)S(1)}, u32[]{:S(2)}, u32[]{:S(2)}) collective-permute-start(bf16[4,12,128,128]{3,2,1,0:T(8,128)(2,1)} %param.5), channel_id=1, source_target_pairs={{0,1},{1,2},{2,3},{4,5},{5,6},{6,7},{8,9},{9,10},{10,11},{12,13},{... | collective-permute-start | bytes 4718600 | tf_op jit(solution)/shard_map/ppermute | solution.py:17
  40.2 38.9 %copy-start.3 = (bf16[4,12,128,128]{3,2,1,0:T(8,128)(2,1)}, bf16[4,12,128,128]{3,2,1,0:T(8,128)(2,1)S(1)}, u32[]{:S(2)}) copy-start(bf16[4,12,128,128]{3,2,1,0:T(8,128)(2,1)S(1)} %collective-permute-done.6) | copy-start | bytes 4718596
  40.2 37.6 %collective-permute-start.7 = (bf16[4,12,128,128]{3,2,1,0:T(8,128)(2,1)S(1)}, bf16[4,12,128,128]{3,2,1,0:T(8,128)(2,1)}, u32[]{:S(2)}, u32[]{:S(2)}) collective-permute-start(bf16[4,12,128,128]{3,2,1,0:T(8,128)(2,1)S(1)} %collective-permute-done.6), channel_id=1, source_target_pairs={{1,0},{2,1},{5,4},{6,5},{9,8},{10,9},{13,12},{14,13},{17,16},{18,1... | collective-permute-start | bytes 4718600 | tf_op jit(solution)/shard_map/ppermute | solution.py:17
  41.5 37.6 %collective-permute-start.5 = (bf16[4,12,128,128]{3,2,1,0:T(8,128)(2,1)S(1)}, bf16[4,12,128,128]{3,2,1,0:T(8,128)(2,1)}, u32[]{:S(2)}, u32[]{:S(2)}) collective-permute-start(bf16[4,12,128,128]{3,2,1,0:T(8,128)(2,1)S(1)} %collective-permute-done.4), channel_id=1, source_target_pairs={{1,2},{2,3},{5,6},{6,7},{9,10},{10,11},{13,14},{14,15},{17,18},{18... | collective-permute-start | bytes 4718600 | tf_op jit(solution)/shard_map/ppermute | solution.py:17
  43.3 1.1 copy-start.1
  77.7 36.9 %collective-permute-start.8 = (bf16[4,12,128,128]{3,2,1,0:T(8,128)(2,1)}, bf16[4,12,128,128]{3,2,1,0:T(8,128)(2,1)}, u32[]{:S(2)}, u32[]{:S(2)}) collective-permute-start(bf16[4,12,128,128]{3,2,1,0:T(8,128)(2,1)} %collective-permute-done.7), channel_id=1, source_target_pairs={{1,0},{5,4},{9,8},{13,12},{17,16},{21,20},{25,24},{29,28}} | collective-permute-start | bytes 4718600 | tf_op jit(solution)/shard_map/ppermute | solution.py:17
  79.0 37.5 %collective-permute-start.11 = (bf16[4,12,128,128]{3,2,1,0:T(8,128)(2,1)}, bf16[4,12,128,128]{3,2,1,0:T(8,128)(2,1)}, u32[]{:S(2)}, u32[]{:S(2)}) collective-permute-start(bf16[4,12,128,128]{3,2,1,0:T(8,128)(2,1)} %collective-permute-done.5), channel_id=1, source_target_pairs={{2,3},{6,7},{10,11},{14,15},{18,19},{22,23},{26,27},{30,31}} | collective-permute-start | bytes 4718600 | tf_op jit(solution)/shard_map/ppermute | solution.py:17
  80.9 58.7 %collective-permute-start.10 = (bf16[4,12,128,128]{3,2,1,0:T(8,128)(2,1)}, bf16[4,12,128,128]{3,2,1,0:T(8,128)(2,1)}, u32[]{:S(2)}, u32[]{:S(2)}) collective-permute-start(bf16[4,12,128,128]{3,2,1,0:T(8,128)(2,1)} %collective-permute-done.7), channel_id=1, source_target_pairs={{28,0},{29,1},{0,4},{1,5},{4,8},{5,9},{8,12},{9,13},{12,16},{13,17... | collective-permute-start | bytes 4718600 | tf_op jit(solution)/shard_map/ppermute | solution.py:17
  82.8 56.8 %collective-permute-start.13 = (bf16[4,12,128,128]{3,2,1,0:T(8,128)(2,1)}, bf16[4,12,128,128]{3,2,1,0:T(8,128)(2,1)}, u32[]{:S(2)}, u32[]{:S(2)}) collective-permute-start(bf16[4,12,128,128]{3,2,1,0:T(8,128)(2,1)} %collective-permute-done.5), channel_id=1, source_target_pairs={{6,2},{7,3},{10,6},{11,7},{14,10},{15,11},{18,14},{19,15},{22,18},... | collective-permute-start | bytes 4718600 | tf_op jit(solution)/shard_map/ppermute | solution.py:17
  114.6 25.0 %collective-permute-start.9 = (bf16[4,12,128,128]{3,2,1,0:T(8,128)(2,1)}, bf16[4,12,128,128]{3,2,1,0:T(8,128)(2,1)}, u32[]{:S(2)}, u32[]{:S(2)}) collective-permute-start(bf16[4,12,128,128]{3,2,1,0:T(8,128)(2,1)} %collective-permute-done.8), channel_id=1, source_target_pairs={{28,0},{0,4},{4,8},{8,12},{12,16},{16,20},{20,24},{24,28}} | collective-permute-start | bytes 4718600 | tf_op jit(solution)/shard_map/ppermute | solution.py:17
  116.5 23.1 %collective-permute-start.12 = (bf16[4,12,128,128]{3,2,1,0:T(8,128)(2,1)}, bf16[4,12,128,128]{3,2,1,0:T(8,128)(2,1)}, u32[]{:S(2)}, u32[]{:S(2)}) collective-permute-start(bf16[4,12,128,128]{3,2,1,0:T(8,128)(2,1)} %collective-permute-done.11), channel_id=1, source_target_pairs={{7,3},{11,7},{15,11},{19,15},{23,19},{27,23},{31,27},{3,31}} | collective-permute-start | bytes 4718600 | tf_op jit(solution)/shard_map/ppermute | solution.py:17
  118.4 6.0 %collective-permute-start = (s32[4,12]{1,0:T(4,128)}, s32[4,12]{1,0:T(4,128)S(1)}, u32[]{:S(2)}, u32[]{:S(2)}) collective-permute-start(s32[4,12]{1,0:T(4,128)} %param.6), channel_id=1, source_target_pairs={{30,0},{31,1},{0,2},{1,3},{2,4},{3,5},{4,6},{5,7},{6,8},{7,9},{8,1... | collective-permute-start | bytes 584 | tf_op jit(solution)/shard_map/ppermute | solution.py:17
  121.4 3.1 %copy-start.4 = (s32[4,12]{1,0:T(4,128)S(1)}, s32[4,12]{1,0:T(4,128)}, u32[]{:S(2)}) copy-start(s32[4,12]{1,0:T(4,128)} %param.6) | copy-start | bytes 580
  123.0 16.6 %copy-start = (bf16[4,12,128,128]{3,2,1,0:T(8,128)(2,1)S(1)}, bf16[4,12,128,128]{3,2,1,0:T(8,128)(2,1)}, u32[]{:S(2)}) copy-start(bf16[4,12,128,128]{3,2,1,0:T(8,128)(2,1)} %param.5) | copy-start | bytes 4718596
  124.5 6.7 %collective-permute-start.1 = (s32[4,12]{1,0:T(4,128)S(1)}, s32[4,12]{1,0:T(4,128)S(1)}, u32[]{:S(2)}, u32[]{:S(2)}) collective-permute-start(s32[4,12]{1,0:T(4,128)S(1)} %copy-done.4), channel_id=1, source_target_pairs={{31,0},{0,1},{1,2},{2,3},{3,4},{4,5},{5,6},{6,7},{7,8},{8,9},{9,10... | collective-permute-start | bytes 584 | tf_op jit(solution)/shard_map/ppermute | solution.py:17
  131.2 3.6 %collective-permute-start.2 = (s32[4,12]{1,0:T(4,128)S(1)}, s32[4,12]{1,0:T(4,128)S(1)}, u32[]{:S(2)}, u32[]{:S(2)}) collective-permute-start(s32[4,12]{1,0:T(4,128)S(1)} %copy-done.4), channel_id=1, source_target_pairs={{1,0},{2,1},{3,2},{4,3},{5,4},{6,5},{7,6},{8,7},{9,8},{10,9},{11,1... | collective-permute-start | bytes 584 | tf_op jit(solution)/shard_map/ppermute | solution.py:17
  134.7 4.5 %collective-permute-start.3 = (s32[4,12]{1,0:T(4,128)S(1)}, s32[4,12]{1,0:T(4,128)S(1)}, u32[]{:S(2)}, u32[]{:S(2)}) collective-permute-start(s32[4,12]{1,0:T(4,128)S(1)} %copy-done.4), channel_id=1, source_target_pairs={{2,0},{3,1},{4,2},{5,3},{6,4},{7,5},{8,6},{9,7},{10,8},{11,9},{12,... | collective-permute-start | bytes 584 | tf_op jit(solution)/shard_map/ppermute | solution.py:17
  139.6 1.4 copy-start.2
  141.0 12.1 %copy-start.5 = (s32[128]{0:T(128)S(1)}, s32[128]{0:T(128)}, u32[]{:S(2)}) copy-start(s32[128]{0:T(128)} %param.9) | copy-start | bytes 1540

commit v2 on v1

--- a/solution.py
+++ b/solution.py
@@ -10,58 +10,58 @@
 AXES = ("layer", "row", "col")
 
 
-def hop(value, distance, keep):
+def fetched(value, offset, keep):
     total = lax.axis_size(AXES)
     line = lax.axis_size("col")
-    route = [((i - distance) % total, i) for i in range(total) if keep(i % line)]
+    route = [((i + offset) % total, i) for i in range(total) if keep(i % line)]
     return lax.ppermute(value, AXES, route)
 
 
-def gathered(block, line):
-    up1 = hop(block, 1, lambda z: z >= 1)
-    down1 = hop(block, -1, lambda z: z <= line - 2)
-    up2 = hop(up1, 1, lambda z: z >= 2)
-    down2 = hop(down1, -1, lambda z: z <= line - 3)
-    up = {1: up1, 2: up2}
-    down = {1: down1, 2: down2}
-    for step in range(3, line):
-        up[step] = hop(up[step - 1], 1, lambda z, step=step: z >= step)
-        down[step] = hop(down[step - 1], -1, lambda z, step=step: z <= line - 1 - step)
-    over_far = hop(up[line - 2], -line, lambda z: z >= line - 2)
-    over_near = hop(up[line - 1], -line, lambda z: z == line - 1)
-    under_far = hop(down[line - 2], line, lambda z: z <= 1)
-    under_near = hop(down[line - 1], line, lambda z: z == 0)
-    return up1, up2, down1, down2, under_near, under_far, over_near, over_far
-
-
-def step_kernel(
-    rows, keep, where_ref, column_ref, place_ref,
-    own, up1, up2, down1, down2, under_near, under_far, over_near, over_far,
-    ham_ref, factor_ref,
-    next_ref, force_ref,
-    held, left, square, product, sems,
-):
+def gathered(parts, line, beside):
+    up1 = [fetched(part, -1, lambda z: z >= 1) for part in parts]
+    down1 = [fetched(part, 1, lambda z: z <= line - 2) for part in parts]
+    up1[-1], down1[-1], beside = lax.optimization_barrier((up1[-1], down1[-1], beside))
+    up2 = [fetched(part, -1, lambda z: z >= 2) for part in up1]
+    down2 = [fetched(part, 1, lambda z: z <= line - 3) for part in down1]
+    brought_up, brought_down = up2, down2
+    for step in range(3, line - 1):
+        brought_up = [fetched(part, -1, lambda z: z >= step) for part in brought_up]
+        brought_down = [fetched(part, 1, lambda z: z <= line - 1 - step) for part in brought_down]
+    over_near = [fetched(part, line - 1, lambda z: z == line - 1) for part in brought_up]
+    under_near = [fetched(part, 1 - line, lambda z: z == 0) for part in brought_down]
+    over_far = [fetched(part, line, lambda z: z >= line - 2) for part in brought_up]
+    under_far = [fetched(part, -line, lambda z: z <= 1) for part in brought_down]
+    return [up1, up2, down1, down2, under_near, under_far, over_near, over_far], beside
+
+
+def step_kernel(rows, keep, cuts, where_ref, column_ref, place_ref, own, *refs):
+    others, (ham_ref, factor_ref, next_ref, force_ref), (held, left, square, product, sems) = (
+        refs[: 8 * cuts], refs[8 * cuts : -5][:4], refs[-5:],
+    )
+    others = [others[g * cuts : (g + 1) * cuts] for g in range(8)]
+    up1, up2, down1, down2, under_near, under_far, over_near, over_far = others
     size = own.shape[2]
     groups = size // 4
     span = 5 * rows
     batch = rows * keep
+    piece = batch // cuts
     z = place_ref[0]
     line = place_ref[1]
 
-    def fetch(part, near, far, condition):
-        spot = held.at[pl.ds(part * batch, batch)]
-
+    def fetch(part, here, there, condition):
         @pl.when(condition)
         def _():
-            pltpu.make_async_copy(near, spot, sems.at[part]).start()
-
-        if far is not None:
-
-            @pl.when(jnp.logical_not(condition))
-            def _():
-                pltpu.make_async_copy(far, spot, sems.at[part]).start()
-
-    fetch(2, own, None, z >= 0)
+            for h in range(cuts):
+                spot = held.at[pl.ds(part * batch + h * piece, piece)]
+                pltpu.make_async_copy(here[h], spot, sems.at[part]).start()
+
+        @pl.when(jnp.logical_not(condition))
+        def _():
+            for h in range(cuts):
+                spot = held.at[pl.ds(part * batch + h * piece, piece)]
+                pltpu.make_async_copy(there[h], spot, sems.at[part]).start()
+
+    pltpu.make_async_copy(own, held.at[pl.ds(2 * batch, batch)], sems.at[2]).start()
     fetch(1, up1, under_near, z >= 1)
     fetch(3, down1, over_near, z <= line - 2)
     fetch(0, up2, under_far, z >= 2)
@@ -131,8 +131,12 @@
     atoms = blocks * groups
     position = lax.axis_index(AXES)
 
-    patterns = {d: hop(pattern, d, lambda z: True) for d in (2, 1, -1, -2)}
-    extended = jnp.concatenate([patterns[2], patterns[1], pattern, patterns[-1], patterns[-2]], axis=0)
+    cuts = 2
+    piece = rows // cuts
+    patterns = {d: fetched(pattern, d, lambda z: True) for d in (-2, -1, 1, 2)}
+    parts = [density[h * piece : (h + 1) * piece] for h in range(cuts)]
+    parts, patterns = lax.optimization_barrier((parts, patterns))
+    extended = jnp.concatenate([patterns[-2], patterns[-1], pattern, patterns[1], patterns[2]], axis=0)
     anchor = position * rows - 2 * rows
     span = 5 * rows
     relative = jnp.where(extended >= 0, jnp.mod(extended - anchor, blocks), -1)
@@ -147,18 +151,19 @@
     factor = factor.reshape(3, rows, keep, groups, size)
     mine = (atom_of_group[:, None] == jnp.arange(atoms, dtype=jnp.int32)[None, :]).astype(jnp.float32)
 
-    near = gathered(density, line)
+    near, (where, columns, factor) = gathered(parts, line, (where, columns, factor))
+    near = [part.reshape(piece * keep, size, size) for parts in near for part in parts]
 
     any_space = pl.BlockSpec(memory_space=pl.ANY)
     vmem = pl.BlockSpec(memory_space=pltpu.VMEM)
     smem = pl.BlockSpec(memory_space=pltpu.SMEM)
     next_density, sums = pl.pallas_call(
-        functools.partial(step_kernel, rows, keep),
+        functools.partial(step_kernel, rows, keep, cuts),
         out_shape=(
             jax.ShapeDtypeStruct(density.shape, density.dtype),
             jax.ShapeDtypeStruct((3, rows, groups, size), jnp.float32),
         ),
-        in_specs=[smem] * 3 + [any_space] * 9 + [vmem] * 2,
+        in_specs=[smem] * 3 + [any_space] * (1 + len(near)) + [vmem] * 2,
         out_specs=(vmem, vmem),
         scratch_shapes=[
             pltpu.VMEM((span * keep + 1, size, size), jnp.bfloat16),
@@ -172,7 +177,8 @@
         where,
         columns,
         place,
-        *[x.reshape(rows * keep, size, size) for x in (density, *near)],
+        density.reshape(rows * keep, size, size),
+        *near,
         ham_derivative,
         factor,
     )

time: 167 us -> 151 us (0.904)
  waiting for transfers between devices: 109 us -> 81.8 us
  starting transfers between devices: 22.9 us -> 33.7 us
  blocking collectives: 11.7 us -> 10 us
    ppermute x14 -> x20, waiting for transfers between devices: 109 us -> 81.8 us  [fetched(): return lax.ppermute(value, AXES, route)]
    ppermute x14 -> x20, starting transfers between devices: 22.9 us -> 33.7 us  [fetched(): return lax.ppermute(value, AXES, route)]
    slice x0 -> x1, local copies, waits for them, and re-layouts: none -> 2.71 us  [on_device(): parts = [density[h * piece:(h + 1) * piece] for h in range(cuts)]]
    unnamed x13 -> x27, local copies, waits for them, and re-layouts: 3.62 us -> 1.49 us
  transfers between devices with their start and end apart: 14 -> 20, of which waited for: 7 -> 9; matrix products, arithmetic and copies ran while one was open for 3% -> 5% of each run, Pallas kernels for 0% -> 0%
where the time goes in v2:
time: 151 us; the launch traced here: 150 us
  waiting for transfers between devices  81.8 us (54%)
  starting transfers between devices  33.7 us (22%)
  Pallas kernels  11.9 us (8%)
  blocking collectives  10 us (7%)
  local copies, waits for them, and re-layouts  7.79 us (5%)
  matrix products  2.95 us (2%)
    ppermute x20, waiting for transfers between devices, fetched(): return lax.ppermute(value, AXES, route)  81.8 us
    ppermute x20, starting transfers between devices, fetched(): return lax.ppermute(value, AXES, route)  33.7 us
    pallas_call x1, Pallas kernels, on_device(): pl.pallas_call(functools.partial(step_kernel, rows, keep, cuts), out_shap...  11.9 us
    all_to_all x1, blocking collectives, on_device(): lax.all_to_all(spread_out.reshape(3, devices, rows * groups), AXES, split...  10 us
  transfers between devices with their start and end apart: 20, of which 9 were waited for; matrix products, arithmetic and copies ran while one was open for 5% of the time, Pallas kernels for 0%

profile of v2, /device:TPU:0, one launch (start us, length us, event | category | flops | bytes accessed | tf_op | source)
XLA Modules:
  0.0 150.0 jit_solution(17267023830086821705)
XLA Ops:
  0.6 4.1 %collective-permute-start = (s32[4,12]{1,0:T(4,128)}, s32[4,12]{1,0:T(4,128)S(1)}, u32[]{:S(2)}, u32[]{:S(2)}) collective-permute-start(s32[4,12]{1,0:T(4,128)} %param.6), channel_id=1, source_target_pairs={{30,0},{31,1},{0,2},{1,3},{2,4},{3,5},{4,6},{5,7},{6,8},{7,9},{8,1... | collective-permute-start | bytes 584 | tf_op jit(solution)/shard_map/ppermute | solution.py:17
  4.7 1.6 %collective-permute-start.1 = (s32[4,12]{1,0:T(4,128)}, s32[4,12]{1,0:T(4,128)S(1)}, u32[]{:S(2)}, u32[]{:S(2)}) collective-permute-start(s32[4,12]{1,0:T(4,128)} %param.6), channel_id=1, source_target_pairs={{31,0},{0,1},{1,2},{2,3},{3,4},{4,5},{5,6},{6,7},{7,8},{8,9},{9,10... | collective-permute-start | bytes 584 | tf_op jit(solution)/shard_map/ppermute | solution.py:17
  6.3 3.8 %collective-permute-start.2 = (s32[4,12]{1,0:T(4,128)}, s32[4,12]{1,0:T(4,128)S(1)}, u32[]{:S(2)}, u32[]{:S(2)}) collective-permute-start(s32[4,12]{1,0:T(4,128)} %param.6), channel_id=1, source_target_pairs={{1,0},{2,1},{3,2},{4,3},{5,4},{6,5},{7,6},{8,7},{9,8},{10,9},{11,1... | collective-permute-start | bytes 584 | tf_op jit(solution)/shard_map/ppermute | solution.py:17
  10.1 2.7 %fusion.7 = (bf16[2,12,128,128]{3,2,1,0:T(8,128)(2,1)}, bf16[2,12,128,128]{3,2,1,0:T(8,128)(2,1)}) fusion(bf16[4,12,128,128]{3,2,1,0:T(8,128)(2,1)} %param.5), kind=kLoop, calls=%fused_computation.17 | loop fusion | bytes 3145728 | tf_op jit(solution)/shard_map/slice | solution.py:137
  12.8 2.0 %collective-permute-done.3 = s32[4,12]{1,0:T(4,128)S(1)} collective-permute-done((s32[4,12]{1,0:T(4,128)}, s32[4,12]{1,0:T(4,128)S(1)}, u32[]{:S(2)}, u32[]{:S(2)}) %collective-permute-start.3) | collective-permute-done | bytes 224 | tf_op jit(solution)/shard_map/ppermute | solution.py:17
  14.8 1.3 collective-permute-start.4
  16.1 1.3 collective-permute-start.5
  18.5 1.5 convolution_bitcast_fusion
  20.0 2.5 %copy.12 = bf16[4608,128]{1,0:T(8,128)(2,1)} copy(bf16[4608,128]{0,1:T(8,128)(2,1)} %convolution_bitcast_fusion) | data formatting | bytes 2359296 | tf_op jit(solution)/shard_map/dot_general | solution.py:150
  23.9 5.3 %collective-permute-start.6 = (bf16[2,12,128,128]{3,2,1,0:T(8,128)(2,1)S(1)}, bf16[2,12,128,128]{3,2,1,0:T(8,128)(2,1)S(1)}, u32[]{:S(2)}, u32[]{:S(2)}) collective-permute-start(bf16[2,12,128,128]{3,2,1,0:T(8,128)(2,1)S(1)} %copy-done.9), channel_id=1, source_target_pairs={{0,1},{1,2},{2,3},{4,5},{5,6},{6,7},{8,9},{9,10},{10,11},{12,13},{... | collective-permute-start | bytes 2359304 | tf_op jit(solution)/shard_map/ppermute | solution.py:17
  29.4 3.5 %collective-permute-done.4 = bf16[2,12,128,128]{3,2,1,0:T(8,128)(2,1)S(1)} collective-permute-done((bf16[2,12,128,128]{3,2,1,0:T(8,128)(2,1)}, bf16[2,12,128,128]{3,2,1,0:T(8,128)(2,1)S(1)}, u32[]{:S(2)}, u32[]{:S(2)}) %collective-permute-start.4) | collective-permute-done | bytes 786464 | tf_op jit(solution)/shard_map/ppermute | solution.py:17
  32.9 5.9 %collective-permute-done.5 = bf16[2,12,128,128]{3,2,1,0:T(8,128)(2,1)S(1)} collective-permute-done((bf16[2,12,128,128]{3,2,1,0:T(8,128)(2,1)}, bf16[2,12,128,128]{3,2,1,0:T(8,128)(2,1)S(1)}, u32[]{:S(2)}, u32[]{:S(2)}) %collective-permute-start.5) | collective-permute-done | bytes 786464 | tf_op jit(solution)/shard_map/ppermute | solution.py:17
  40.8 14.8 %collective-permute-done.9 = bf16[2,12,128,128]{3,2,1,0:T(8,128)(2,1)S(1)} collective-permute-done((bf16[2,12,128,128]{3,2,1,0:T(8,128)(2,1)S(1)}, bf16[2,12,128,128]{3,2,1,0:T(8,128)(2,1)S(1)}, u32[]{:S(2)}, u32[]{:S(2)}) %collective-permute-start.9) | collective-permute-done | bytes 786464 | tf_op jit(solution)/shard_map/ppermute | solution.py:17
  57.7 14.8 %collective-permute-done.11 = bf16[2,12,128,128]{3,2,1,0:T(8,128)(2,1)S(1)} collective-permute-done((bf16[2,12,128,128]{3,2,1,0:T(8,128)(2,1)S(1)}, bf16[2,12,128,128]{3,2,1,0:T(8,128)(2,1)S(1)}, u32[]{:S(2)}, u32[]{:S(2)}) %collective-permute-start.11) | collective-permute-done | bytes 786464 | tf_op jit(solution)/shard_map/ppermute | solution.py:17
  73.8 1.9 %collective-permute-start.15 = (bf16[2,12,128,128]{3,2,1,0:T(8,128)(2,1)S(1)}, bf16[2,12,128,128]{3,2,1,0:T(8,128)(2,1)S(1)}, u32[]{:S(2)}, u32[]{:S(2)}) collective-permute-start(bf16[2,12,128,128]{3,2,1,0:T(8,128)(2,1)S(1)} %collective-permute-done.11), channel_id=1, source_target_pairs={{28,0},{29,1},{0,4},{1,5},{4,8},{5,9},{8,12},{9,13},{12,16},{13,17... | collective-permute-start | bytes 2359304 | tf_op jit(solution)/shard_map/ppermute | solution.py:17
  76.4 12.9 %collective-permute-done.10 = bf16[2,12,128,128]{3,2,1,0:T(8,128)(2,1)S(1)} collective-permute-done((bf16[2,12,128,128]{3,2,1,0:T(8,128)(2,1)S(1)}, bf16[2,12,128,128]{3,2,1,0:T(8,128)(2,1)S(1)}, u32[]{:S(2)}, u32[]{:S(2)}) %collective-permute-start.10) | collective-permute-done | bytes 786464 | tf_op jit(solution)/shard_map/ppermute | solution.py:17
  90.1 1.3 collective-permute-start.12
  91.4 13.2 %collective-permute-done.13 = bf16[2,12,128,128]{3,2,1,0:T(8,128)(2,1)S(1)} collective-permute-done((bf16[2,12,128,128]{3,2,1,0:T(8,128)(2,1)S(1)}, bf16[2,12,128,128]{3,2,1,0:T(8,128)(2,1)S(1)}, u32[]{:S(2)}, u32[]{:S(2)}) %collective-permute-start.13) | collective-permute-done | bytes 786464 | tf_op jit(solution)/shard_map/ppermute | solution.py:17
  104.5 3.7 %collective-permute-start.14 = (bf16[2,12,128,128]{3,2,1,0:T(8,128)(2,1)S(1)}, bf16[2,12,128,128]{3,2,1,0:T(8,128)(2,1)S(1)}, u32[]{:S(2)}, u32[]{:S(2)}) collective-permute-start(bf16[2,12,128,128]{3,2,1,0:T(8,128)(2,1)S(1)} %collective-permute-done.10), channel_id=1, source_target_pairs={{28,0},{29,1},{0,4},{1,5},{4,8},{5,9},{8,12},{9,13},{12,16},{13,17... | collective-permute-start | bytes 2359304 | tf_op jit(solution)/shard_map/ppermute | solution.py:17
  109.8 11.6 %collective-permute-done.12 = bf16[2,12,128,128]{3,2,1,0:T(8,128)(2,1)S(1)} collective-permute-done((bf16[2,12,128,128]{3,2,1,0:T(8,128)(2,1)S(1)}, bf16[2,12,128,128]{3,2,1,0:T(8,128)(2,1)S(1)}, u32[]{:S(2)}, u32[]{:S(2)}) %collective-permute-start.12) | collective-permute-done | bytes 786464 | tf_op jit(solution)/shard_map/ppermute | solution.py:17
  121.4 3.0 %collective-permute-done.14 = bf16[2,12,128,128]{3,2,1,0:T(8,128)(2,1)S(1)} collective-permute-done((bf16[2,12,128,128]{3,2,1,0:T(8,128)(2,1)S(1)}, bf16[2,12,128,128]{3,2,1,0:T(8,128)(2,1)S(1)}, u32[]{:S(2)}, u32[]{:S(2)}) %collective-permute-start.14) | collective-permute-done | bytes 786464 | tf_op jit(solution)/shard_map/ppermute | solution.py:17
  125.8 11.9 %shard_map.68 = (bf16[4,12,128,128]{3,2,1,0:T(8,128)(2,1)}, f32[3,4,32,128]{3,2,1,0:T(8,128)S(1)}) custom-call(s32[20,20]{1,0:T(8,128)S(1)} %select_reduce_fusion.where_ref, s32[4,12]{1,0:T(4,128)S(1)} %slice.12.column_ref, s32[2]{0:T(128)S(1)} %pad_add_fusion.place_ref, bf16[48,128,128]{2,1,0:T(8,128)(2,1)} %bitcast.32, bf16[24,128,128]{2,1,0:T(8,128)(2,1)S(1)} %bitcast.28, ...), custom_call_target="tpu_custom_call" | custom-call | tf_op jit(solution)/shard_map/pallas_call | solution.py:160
  138.0 1.5 fusion
  139.4 10.0 %all_to_all.5 = f32[3,32,128]{2,0,1:T(4,128)S(1)} all-to-all(f32[3,32,128]{2,0,1:T(4,128)S(1)} %fusion), channel_id=1, replica_groups=mesh['layer'=2,'row'=4,'col'=4] {'layer','row','col'}, dimensions={1} | all-to-all | bytes 98304 | tf_op jit(solution)/shard_map/all_to_all | solution.py:187
  (63 shorter events, 13.0 us)
Async XLA Ops:
  0.6 16.8 %copy-start.10 = (bf16[3,4,12,1024]{3,1,2,0:T(4,128)(2,1)S(1)}, bf16[3,4,12,1024]{3,1,2,0:T(4,128)(2,1)}, u32[]{:S(2)}) copy-start(bf16[3,4,12,1024]{3,1,2,0:T(4,128)(2,1)} %param.8) | copy-start | bytes 884740
  0.6 12.2 %collective-permute-start = (s32[4,12]{1,0:T(4,128)}, s32[4,12]{1,0:T(4,128)S(1)}, u32[]{:S(2)}, u32[]{:S(2)}) collective-permute-start(s32[4,12]{1,0:T(4,128)} %param.6), channel_id=1, source_target_pairs={{30,0},{31,1},{0,2},{1,3},{2,4},{3,5},{4,6},{5,7},{6,8},{7,9},{8,1... | collective-permute-start | bytes 584 | tf_op jit(solution)/shard_map/ppermute | solution.py:17
  4.7 8.1 %collective-permute-start.1 = (s32[4,12]{1,0:T(4,128)}, s32[4,12]{1,0:T(4,128)S(1)}, u32[]{:S(2)}, u32[]{:S(2)}) collective-permute-start(s32[4,12]{1,0:T(4,128)} %param.6), channel_id=1, source_target_pairs={{31,0},{0,1},{1,2},{2,3},{3,4},{4,5},{5,6},{6,7},{7,8},{8,9},{9,10... | collective-permute-start | bytes 584 | tf_op jit(solution)/shard_map/ppermute | solution.py:17
  6.3 6.5 %collective-permute-start.2 = (s32[4,12]{1,0:T(4,128)}, s32[4,12]{1,0:T(4,128)S(1)}, u32[]{:S(2)}, u32[]{:S(2)}) collective-permute-start(s32[4,12]{1,0:T(4,128)} %param.6), channel_id=1, source_target_pairs={{1,0},{2,1},{3,2},{4,3},{5,4},{6,5},{7,6},{8,7},{9,8},{10,9},{11,1... | collective-permute-start | bytes 584 | tf_op jit(solution)/shard_map/ppermute | solution.py:17
  10.1 4.7 %collective-permute-start.3 = (s32[4,12]{1,0:T(4,128)}, s32[4,12]{1,0:T(4,128)S(1)}, u32[]{:S(2)}, u32[]{:S(2)}) collective-permute-start(s32[4,12]{1,0:T(4,128)} %param.6), channel_id=1, source_target_pairs={{2,0},{3,1},{4,2},{5,3},{6,4},{7,5},{8,6},{9,7},{10,8},{11,9},{12,... | collective-permute-start | bytes 584 | tf_op jit(solution)/shard_map/ppermute | solution.py:17
  14.8 18.1 %collective-permute-start.4 = (bf16[2,12,128,128]{3,2,1,0:T(8,128)(2,1)}, bf16[2,12,128,128]{3,2,1,0:T(8,128)(2,1)S(1)}, u32[]{:S(2)}, u32[]{:S(2)}) collective-permute-start(bf16[2,12,128,128]{3,2,1,0:T(8,128)(2,1)} %get-tuple-element.15), channel_id=1, source_target_pairs={{0,1},{1,2},{2,3},{4,5},{5,6},{6,7},{8,9},{9,10},{10,11},{12,13},{... | collective-permute-start | bytes 2359304 | tf_op jit(solution)/shard_map/ppermute | solution.py:17
  16.1 22.7 %collective-permute-start.5 = (bf16[2,12,128,128]{3,2,1,0:T(8,128)(2,1)}, bf16[2,12,128,128]{3,2,1,0:T(8,128)(2,1)S(1)}, u32[]{:S(2)}, u32[]{:S(2)}) collective-permute-start(bf16[2,12,128,128]{3,2,1,0:T(8,128)(2,1)} %get-tuple-element.15), channel_id=1, source_target_pairs={{1,0},{2,1},{3,2},{5,4},{6,5},{7,6},{9,8},{10,9},{11,10},{13,12},{... | collective-permute-start | bytes 2359304 | tf_op jit(solution)/shard_map/ppermute | solution.py:17
  22.6 33.0 %collective-permute-start.9 = (bf16[2,12,128,128]{3,2,1,0:T(8,128)(2,1)S(1)}, bf16[2,12,128,128]{3,2,1,0:T(8,128)(2,1)S(1)}, u32[]{:S(2)}, u32[]{:S(2)}) collective-permute-start(bf16[2,12,128,128]{3,2,1,0:T(8,128)(2,1)S(1)} %copy-done.9), channel_id=1, source_target_pairs={{1,0},{2,1},{3,2},{5,4},{6,5},{7,6},{9,8},{10,9},{11,10},{13,12},{... | collective-permute-start | bytes 2359304 | tf_op jit(solution)/shard_map/ppermute | solution.py:17
  23.9 33.0 %collective-permute-start.6 = (bf16[2,12,128,128]{3,2,1,0:T(8,128)(2,1)S(1)}, bf16[2,12,128,128]{3,2,1,0:T(8,128)(2,1)S(1)}, u32[]{:S(2)}, u32[]{:S(2)}) collective-permute-start(bf16[2,12,128,128]{3,2,1,0:T(8,128)(2,1)S(1)} %copy-done.9), channel_id=1, source_target_pairs={{0,1},{1,2},{2,3},{4,5},{5,6},{6,7},{8,9},{9,10},{10,11},{12,13},{... | collective-permute-start | bytes 2359304 | tf_op jit(solution)/shard_map/ppermute | solution.py:17
  38.8 33.7 %collective-permute-start.11 = (bf16[2,12,128,128]{3,2,1,0:T(8,128)(2,1)S(1)}, bf16[2,12,128,128]{3,2,1,0:T(8,128)(2,1)S(1)}, u32[]{:S(2)}, u32[]{:S(2)}) collective-permute-start(bf16[2,12,128,128]{3,2,1,0:T(8,128)(2,1)S(1)} %collective-permute-done.5), channel_id=1, source_target_pairs={{1,0},{2,1},{5,4},{6,5},{9,8},{10,9},{13,12},{14,13},{17,16},{18,1... | collective-permute-start | bytes 2359304 | tf_op jit(solution)/shard_map/ppermute | solution.py:17
  40.1 35.6 %collective-permute-start.8 = (bf16[2,12,128,128]{3,2,1,0:T(8,128)(2,1)S(1)}, bf16[2,12,128,128]{3,2,1,0:T(8,128)(2,1)S(1)}, u32[]{:S(2)}, u32[]{:S(2)}) collective-permute-start(bf16[2,12,128,128]{3,2,1,0:T(8,128)(2,1)S(1)} %collective-permute-done.4), channel_id=1, source_target_pairs={{1,2},{2,3},{5,6},{6,7},{9,10},{10,11},{13,14},{14,15},{17,18},{18... | collective-permute-start | bytes 2359304 | tf_op jit(solution)/shard_map/ppermute | solution.py:17
  55.6 33.7 %collective-permute-start.10 = (bf16[2,12,128,128]{3,2,1,0:T(8,128)(2,1)S(1)}, bf16[2,12,128,128]{3,2,1,0:T(8,128)(2,1)S(1)}, u32[]{:S(2)}, u32[]{:S(2)}) collective-permute-start(bf16[2,12,128,128]{3,2,1,0:T(8,128)(2,1)S(1)} %collective-permute-done.9), channel_id=1, source_target_pairs={{1,0},{2,1},{5,4},{6,5},{9,8},{10,9},{13,12},{14,13},{17,16},{18,1... | collective-permute-start | bytes 2359304 | tf_op jit(solution)/shard_map/ppermute | solution.py:17
  56.9 33.1 %collective-permute-start.7 = (bf16[2,12,128,128]{3,2,1,0:T(8,128)(2,1)S(1)}, bf16[2,12,128,128]{3,2,1,0:T(8,128)(2,1)S(1)}, u32[]{:S(2)}, u32[]{:S(2)}) collective-permute-start(bf16[2,12,128,128]{3,2,1,0:T(8,128)(2,1)S(1)} %collective-permute-done.6), channel_id=1, source_target_pairs={{1,2},{2,3},{5,6},{6,7},{9,10},{10,11},{13,14},{14,15},{17,18},{18... | collective-permute-start | bytes 2359304 | tf_op jit(solution)/shard_map/ppermute | solution.py:17
  72.5 51.9 %copy-start = (bf16[2,12,128,128]{3,2,1,0:T(8,128)(2,1)}, bf16[2,12,128,128]{3,2,1,0:T(8,128)(2,1)S(1)}, u32[]{:S(2)}) copy-start(bf16[2,12,128,128]{3,2,1,0:T(8,128)(2,1)S(1)} %collective-permute-done.11) | copy-start | bytes 2359300
  72.5 32.0 %collective-permute-start.13 = (bf16[2,12,128,128]{3,2,1,0:T(8,128)(2,1)S(1)}, bf16[2,12,128,128]{3,2,1,0:T(8,128)(2,1)S(1)}, u32[]{:S(2)}, u32[]{:S(2)}) collective-permute-start(bf16[2,12,128,128]{3,2,1,0:T(8,128)(2,1)S(1)} %collective-permute-done.11), channel_id=1, source_target_pairs={{29,0},{1,4},{5,8},{9,12},{13,16},{17,20},{21,24},{25,28}} | collective-permute-start | bytes 2359304 | tf_op jit(solution)/shard_map/ppermute | solution.py:17
  73.8 34.4 %collective-permute-start.15 = (bf16[2,12,128,128]{3,2,1,0:T(8,128)(2,1)S(1)}, bf16[2,12,128,128]{3,2,1,0:T(8,128)(2,1)S(1)}, u32[]{:S(2)}, u32[]{:S(2)}) collective-permute-start(bf16[2,12,128,128]{3,2,1,0:T(8,128)(2,1)S(1)} %collective-permute-done.11), channel_id=1, source_target_pairs={{28,0},{29,1},{0,4},{1,5},{4,8},{5,9},{8,12},{9,13},{12,16},{13,17... | collective-permute-start | bytes 2359304 | tf_op jit(solution)/shard_map/ppermute | solution.py:17
  75.7 33.2 %collective-permute-start.17 = (bf16[2,12,128,128]{3,2,1,0:T(8,128)(2,1)S(1)}, bf16[2,12,128,128]{3,2,1,0:T(8,128)(2,1)S(1)}, u32[]{:S(2)}, u32[]{:S(2)}) collective-permute-start(bf16[2,12,128,128]{3,2,1,0:T(8,128)(2,1)S(1)} %collective-permute-done.8), channel_id=1, source_target_pairs={{6,3},{10,7},{14,11},{18,15},{22,19},{26,23},{30,27},{2,31}} | collective-permute-start | bytes 2359304 | tf_op jit(solution)/shard_map/ppermute | solution.py:17
  89.3 20.4 %collective-permute-start.19 = (bf16[2,12,128,128]{3,2,1,0:T(8,128)(2,1)S(1)}, bf16[2,12,128,128]{3,2,1,0:T(8,128)(2,1)S(1)}, u32[]{:S(2)}, u32[]{:S(2)}) collective-permute-start(bf16[2,12,128,128]{3,2,1,0:T(8,128)(2,1)S(1)} %collective-permute-done.8), channel_id=1, source_target_pairs={{6,2},{7,3},{10,6},{11,7},{14,10},{15,11},{18,14},{19,15},{22,18},... | collective-permute-start | bytes 2359304 | tf_op jit(solution)/shard_map/ppermute | solution.py:17
  90.1 31.3 %collective-permute-start.12 = (bf16[2,12,128,128]{3,2,1,0:T(8,128)(2,1)S(1)}, bf16[2,12,128,128]{3,2,1,0:T(8,128)(2,1)S(1)}, u32[]{:S(2)}, u32[]{:S(2)}) collective-permute-start(bf16[2,12,128,128]{3,2,1,0:T(8,128)(2,1)S(1)} %collective-permute-done.10), channel_id=1, source_target_pairs={{29,0},{1,4},{5,8},{9,12},{13,16},{17,20},{21,24},{25,28}} | collective-permute-start | bytes 2359304 | tf_op jit(solution)/shard_map/ppermute | solution.py:17
  104.5 19.9 %copy-start.1 = (bf16[2,12,128,128]{3,2,1,0:T(8,128)(2,1)}, bf16[2,12,128,128]{3,2,1,0:T(8,128)(2,1)S(1)}, u32[]{:S(2)}) copy-start(bf16[2,12,128,128]{3,2,1,0:T(8,128)(2,1)S(1)} %collective-permute-done.13) | copy-start | bytes 2359300
  104.5 19.9 %collective-permute-start.14 = (bf16[2,12,128,128]{3,2,1,0:T(8,128)(2,1)S(1)}, bf16[2,12,128,128]{3,2,1,0:T(8,128)(2,1)S(1)}, u32[]{:S(2)}, u32[]{:S(2)}) collective-permute-start(bf16[2,12,128,128]{3,2,1,0:T(8,128)(2,1)S(1)} %collective-permute-done.10), channel_id=1, source_target_pairs={{28,0},{29,1},{0,4},{1,5},{4,8},{5,9},{8,12},{9,13},{12,16},{13,17... | collective-permute-start | bytes 2359304 | tf_op jit(solution)/shard_map/ppermute | solution.py:17
  108.2 16.2 %copy-start.2 = (bf16[2,12,128,128]{3,2,1,0:T(8,128)(2,1)}, bf16[2,12,128,128]{3,2,1,0:T(8,128)(2,1)S(1)}, u32[]{:S(2)}) copy-start(bf16[2,12,128,128]{3,2,1,0:T(8,128)(2,1)S(1)} %collective-permute-done.15) | copy-start | bytes 2359300
  108.2 16.2 %collective-permute-start.16 = (bf16[2,12,128,128]{3,2,1,0:T(8,128)(2,1)S(1)}, bf16[2,12,128,128]{3,2,1,0:T(8,128)(2,1)S(1)}, u32[]{:S(2)}, u32[]{:S(2)}) collective-permute-start(bf16[2,12,128,128]{3,2,1,0:T(8,128)(2,1)S(1)} %collective-permute-done.7), channel_id=1, source_target_pairs={{6,3},{10,7},{14,11},{18,15},{22,19},{26,23},{30,27},{2,31}} | collective-permute-start | bytes 2359304 | tf_op jit(solution)/shard_map/ppermute | solution.py:17
  109.0 15.4 %collective-permute-start.18 = (bf16[2,12,128,128]{3,2,1,0:T(8,128)(2,1)S(1)}, bf16[2,12,128,128]{3,2,1,0:T(8,128)(2,1)S(1)}, u32[]{:S(2)}, u32[]{:S(2)}) collective-permute-start(bf16[2,12,128,128]{3,2,1,0:T(8,128)(2,1)S(1)} %collective-permute-done.7), channel_id=1, source_target_pairs={{6,2},{7,3},{10,6},{11,7},{14,10},{15,11},{18,14},{19,15},{22,18},... | collective-permute-start | bytes 2359304 | tf_op jit(solution)/shard_map/ppermute | solution.py:17
  (9 other events, 54.0 us)

commit v3 on v1

v3 whole, which is shorter than its diff:
```python
import functools

import jax
import jax.numpy as jnp
from jax import lax
from jax.experimental import pallas as pl
from jax.experimental.pallas import tpu as pltpu
from jax.sharding import PartitionSpec as P

AXES = ("layer", "row", "col")
UNUSED = 64
TAIL = 16


def fetched(value, offset, keep):
    total = lax.axis_size(AXES)
    line = lax.axis_size("col")
    route = [((i + offset) % total, i) for i in range(total) if keep(i % line)]
    return lax.ppermute(value, AXES, route)


def early_kernel(rows, keep, where_ref, column_ref, place_ref, own, *refs):
    near, (mixture_out, late_out, held, left, square, mixture_ref, late_ref, sems, out_sems) = refs[:8], refs[8:]
    near = [near[g : g + 2] for g in range(0, 8, 2)]
    size = own.shape[1]
    span = 5 * rows
    height = rows * keep * size
    half = height // 2
    z = place_ref[0]
    line = place_ref[1]
    sources = (
        (0, near[1], z >= 2),
        (1, near[0], z >= 1),
        (3, near[2], z <= line - 2),
        (4, near[3], z <= line - 3),
    )

    def copies(part, pair):
        return [
            pltpu.make_async_copy(
                pair[h].at[pl.ds(0, half)],
                held.at[pl.ds(part * height + h * half, half)],
                sems.at[part, h],
            )
            for h in range(2)
        ]

    mine = pltpu.make_async_copy(own, held.at[pl.ds(2 * height, height)], sems.at[2, 0])
    mine.start()
    for part, pair, valid in sources:

        @pl.when(valid)
        def _(part=part, pair=pair):
            for copy in copies(part, pair):
                copy.start()

    held[pl.ds(5 * height, size)] = jnp.zeros((size, size), held.dtype)
    left[...] = jnp.zeros(left.shape, left.dtype)
    mine.wait()
    for i in range(rows):
        for l in range(keep):
            column = column_ref[i, l]

            @pl.when(column >= 0)
            def _(i=i, l=l, column=column):
                at = pl.multiple_of(column * size, size)
                block = held[pl.ds(2 * height + (i * keep + l) * size, size)]
                left[i * size : (i + 1) * size, pl.ds(at, size)] = block

    width = late_ref.shape[1]
    start = pl.multiple_of(jnp.where(z <= 1, 0, span * size - width), size)
    late_ref[...] = left[:, pl.ds(start, width)]
    put_left = pltpu.make_async_copy(late_ref, late_out, out_sems.at[rows])
    put_left.start()
    for part, pair, valid in sources:

        @pl.when(valid)
        def _(part=part, pair=pair):
            for copy in copies(part, pair):
                copy.wait()

    reach = 2 * rows
    for j in range(0, span, 2):
        low, high = max(0, j - reach), min(span, j + 2 + reach)

        def block(r, c):
            return held[pl.ds(pl.multiple_of(where_ref[r, c] * size, size), size)]

        right = jnp.concatenate(
            [jnp.concatenate([block(r, j), block(r, j + 1)], axis=1) for r in range(low, high)], axis=0
        )
        total = jnp.dot(left[:, low * size : high * size], right, preferred_element_type=jnp.float32)
        square[j] = total[:, :size]
        square[j + 1] = total[:, size:]

    put_mixture = []
    for i in range(rows):

        @pl.loop(0, keep)
        def _(k, i=i):
            column = column_ref[i, k]
            term = square[jnp.maximum(column, 0), i * size : (i + 1) * size, :]
            term = jnp.where(column >= 0, term, 0.0)
            at = pl.multiple_of(2 * height + (i * keep + k) * size, size)
            mixture_ref[i, k] = 2.0 * held[pl.ds(at, size)].astype(jnp.float32) - term

        put_mixture.append(pltpu.make_async_copy(mixture_ref.at[i], mixture_out.at[i], out_sems.at[i]))
        put_mixture[i].start()
    put_left.wait()
    for put in put_mixture:
        put.wait()


def late_kernel(rows, keep, where_ref, column_ref, place_ref, *refs):
    left_in, near_a, near_b, far_a, far_b, mixture_in, ham_in, factor_in, next_out, force_ref = refs[:10]
    left, held, mixture_ref, ham_ref, factor_ref, next_ref, square, product, sems, out_sems = refs[10:]
    size = ham_ref.shape[2]
    groups = size // 4
    span = 5 * rows
    reach = 2 * rows
    height = rows * keep * size
    half = height // 2
    low = place_ref[0] <= 1
    near_at = pl.multiple_of(jnp.where(low, height, 0), size)
    far_at = pl.multiple_of(jnp.where(low, 0, height), size)
    routes = [(left_in, left)]
    for there, at in ((far_a, far_at), (near_a, near_at), (far_b, far_at + half), (near_b, near_at + half)):
        routes.append((there.at[pl.ds(0, half)], held.at[pl.ds(pl.multiple_of(at, size), half)]))
    routes += [(mixture_in, mixture_ref), (ham_in, ham_ref), (factor_in, factor_ref)]
    gets = [pltpu.make_async_copy(there, here, sems.at[n]) for n, (there, here) in enumerate(routes)]
    for get in gets:
        get.start()
    held[pl.ds(2 * height, size)] = jnp.zeros((size, size), held.dtype)
    for get in gets[:5]:
        get.wait()

    def block(r, c):
        return held[pl.ds(pl.multiple_of(where_ref[r, c] * size, size), size)]

    for j in range(0, 2 * reach, 2):
        right = jnp.concatenate(
            [jnp.concatenate([block(r, j), block(r, j + 1)], axis=1) for r in range(reach)], axis=0
        )
        total = jnp.dot(left[...], right, preferred_element_type=jnp.float32)
        square[j] = total[:, :size]
        square[j + 1] = total[:, size:]

    for get in gets[5:]:
        get.wait()
    offset = jnp.where(low, 0, span - 2 * reach)
    puts = []
    for i in range(rows):

        def slot(k, sums, i=i):
            column = column_ref[i, k]
            place = column - offset
            inside = (column >= 0) & (place >= 0) & (place < 2 * reach)
            term = square[jnp.where(inside, place, 0), i * size : (i + 1) * size, :]
            mixture = mixture_ref[i, k] - jnp.where(inside, term, 0.0)
            next_ref[i, k] = mixture.astype(next_ref.dtype)
            product[...] = mixture * ham_ref[i, k].astype(jnp.float32)
            energy = product[pl.ds(0, groups, stride=4), :]
            for r in range(1, 4):
                energy = energy + product[pl.ds(r, groups, stride=4), :]
            return tuple(sums[d] + energy * factor_ref[d, i, k].astype(jnp.float32) for d in range(3))

        start = tuple(jnp.zeros((groups, size), jnp.float32) for _ in range(3))
        sums = lax.fori_loop(0, keep, slot, start)
        puts.append(pltpu.make_async_copy(next_ref.at[i], next_out.at[i], out_sems.at[i]))
        puts[i].start()
        for d in range(3):
            force_ref[d, i] = sums[d]
    for put in puts:
        put.wait()


def on_device(density, pattern, ham_derivative, pair_direction, atom_of_group):
    rows, keep, size, _ = density.shape
    groups = size // 4
    devices = lax.axis_size(AXES)
    line = lax.axis_size("col")
    blocks = rows * devices
    atoms = blocks * groups
    reach = 2 * rows
    span = 5 * rows
    position = lax.axis_index(AXES)
    z = lax.axis_index("col")

    row_at = jnp.arange(span, dtype=jnp.int32)[:, None]
    distance = jnp.mod(pattern - (position * rows + row_at[:rows]) + reach, blocks) - reach
    distance = jnp.where(pattern >= 0, distance, UNUSED)
    tail = jnp.pad(distance.astype(jnp.bfloat16), ((0, TAIL - rows), (0, size - keep)))

    flat = density.reshape(rows * keep * size, size)
    half = rows * keep * size // 2
    parts = [jnp.concatenate([flat[:half], tail], axis=0), jnp.pad(flat[half:], ((0, 2 * TAIL), (0, 0)))]

    def columns_of(pieces):
        return jnp.concatenate([x[half : half + rows, :keep].astype(jnp.int32) for x in pieces], axis=0)

    def steps(part):
        up1 = fetched(part, -1, lambda z: z >= 1)
        down1 = fetched(part, 1, lambda z: z <= line - 2)
        up2 = fetched(up1, -1, lambda z: z >= 2)
        down2 = fetched(down1, 1, lambda z: z <= line - 3)
        brought_up, brought_down = up2, down2
        for step in range(3, line - 1):
            brought_up = fetched(brought_up, -1, lambda z: z >= step)
            brought_down = fetched(brought_down, 1, lambda z: z <= line - 1 - step)
        brought = jnp.where(z >= line - 2, brought_up, brought_down)
        total = line * lax.axis_size(("layer", "row"))
        over = [((i + line - 1) % total, i) for i in range(total) if i % line == line - 1]
        under = [((i + 1 - line) % total, i) for i in range(total) if i % line == 0]
        near = lax.ppermute(brought, AXES, over + under)
        over = [((i + line) % total, i) for i in range(total) if i % line >= line - 2]
        under = [((i - line) % total, i) for i in range(total) if i % line <= 1]
        far = lax.ppermute(brought, AXES, over + under)
        return (up1, up2, down1, down2), near, far

    line_a, near_a, far_a = steps(parts[0])
    line_b, near_b, far_b = steps(parts[1])

    group = row_at // rows
    known = ((group != 0) | (z >= 2)) & ((group != 1) | (z >= 1))
    known = known & ((group != 3) | (z <= line - 2)) & ((group != 4) | (z <= line - 3))
    up, down = columns_of([line_a[1], line_a[0]]), columns_of(line_a[2:])
    extended = jnp.concatenate([up, distance, down], axis=0)
    extended = jnp.where(known & (extended != UNUSED), extended + row_at, -1)
    hit = extended[:, :, None] == jnp.arange(span, dtype=jnp.int32)[None, None, :]
    flat_slot = jnp.arange(span * keep, dtype=jnp.int32).reshape(span, keep, 1)
    where_early = jnp.min(jnp.where(hit, flat_slot, span * keep), axis=1)
    columns = jnp.where(distance != UNUSED, distance + reach + row_at[:rows], -1)

    low = z <= 1
    late = columns_of([far_a, near_a, far_a])
    late = jnp.where(low, late[:reach], late[rows : rows + reach])
    group = row_at[:reach] // rows
    known = jnp.where(low, (group == 0) | (z == 0), jnp.where(group == 0, z == line - 1, z >= line - 2))
    first = jnp.where(low, 0, reach)
    late = jnp.where(known & (late != UNUSED), late + first + row_at[:reach], -1)
    hit = late[:, :, None] == jnp.arange(2 * reach, dtype=jnp.int32)[None, None, :]
    where_late = jnp.min(jnp.where(hit, flat_slot[:reach], reach * keep), axis=1)
    place = jnp.stack([z, jnp.int32(line)]).astype(jnp.int32)

    spread = jnp.repeat(jnp.eye(groups, dtype=jnp.bfloat16), 4, axis=1)
    factor = jnp.dot(pair_direction.reshape(3 * rows * keep * groups, groups), spread)
    factor = factor.reshape(3, rows, keep, groups, size)

    hbm = pl.BlockSpec(memory_space=pltpu.HBM)
    vmem = pl.BlockSpec(memory_space=pltpu.VMEM)
    smem = pl.BlockSpec(memory_space=pltpu.SMEM)
    limit = pltpu.CompilerParams(vmem_limit_bytes=60 * 1024 * 1024)
    mixture, left = pl.pallas_call(
        functools.partial(early_kernel, rows, keep),
        out_shape=(
            jax.ShapeDtypeStruct(density.shape, jnp.float32),
            jax.ShapeDtypeStruct((rows * size, reach * size), jnp.bfloat16),
        ),
        in_specs=[smem] * 3 + [hbm] * 9,
        out_specs=(hbm, hbm),
        scratch_shapes=[
            pltpu.VMEM(((span * keep + 1) * size, size), jnp.bfloat16),
            pltpu.VMEM((rows * size, span * size), jnp.bfloat16),
            pltpu.VMEM((span, rows * size, size), jnp.float32),
            pltpu.VMEM(density.shape, jnp.float32),
            pltpu.VMEM((rows * size, reach * size), jnp.bfloat16),
            pltpu.SemaphoreType.DMA((5, 2)),
            pltpu.SemaphoreType.DMA((rows + 1,)),
        ],
        compiler_params=limit,
        name="early",
    )(where_early, columns, place, flat, *[x for pair in zip(line_a, line_b) for x in pair])
    next_density, sums = pl.pallas_call(
        functools.partial(late_kernel, rows, keep),
        out_shape=(
            jax.ShapeDtypeStruct(density.shape, density.dtype),
            jax.ShapeDtypeStruct((3, rows, groups, size), jnp.float32),
        ),
        in_specs=[smem] * 3 + [hbm] * 8,
        out_specs=(hbm, vmem),
        scratch_shapes=[
            pltpu.VMEM(left.shape, left.dtype),
            pltpu.VMEM(((reach * keep + 1) * size, size), jnp.bfloat16),
            pltpu.VMEM(mixture.shape, mixture.dtype),
            pltpu.VMEM(ham_derivative.shape, ham_derivative.dtype),
            pltpu.VMEM(factor.shape, factor.dtype),
            pltpu.VMEM(density.shape, density.dtype),
            pltpu.VMEM((2 * reach, rows * size, size), jnp.float32),
            pltpu.VMEM((size, size), jnp.float32),
            pltpu.SemaphoreType.DMA((8,)),
            pltpu.SemaphoreType.DMA((rows,)),
        ],
        compiler_params=limit,
        name="late",
    )(where_late, columns, place, left, near_a, near_b, far_a, far_b, mixture, ham_derivative, factor)
    force = jnp.sum(sums, axis=3).reshape(3, rows * groups)
    mine = (atom_of_group[:, None] == jnp.arange(atoms, dtype=jnp.int32)[None, :]).astype(jnp.float32)
    spread_out = jnp.dot(force, mine, precision=lax.Precision.HIGHEST)
    pieces = lax.all_to_all(
        spread_out.reshape(3, devices, rows * groups), AXES, split_axis=1, concat_axis=1, tiled=True
    )
    return next_density, jnp.sum(pieces, axis=1)


def solution(mesh):
    spread = P(AXES, None, None, None)
    return jax.shard_map(
        on_device,
        mesh=mesh,
        in_specs=(spread, P(AXES, None), spread, P(None, AXES, None, None), P(AXES)),
        out_specs=(spread, P(None, AXES)),
        check_vma=False,
    )
```

time: 167 us -> 140 us (0.84)
  waiting for transfers between devices: 109 us -> 67.3 us
  other arithmetic: 1 us -> 10.3 us
  Pallas kernels: 11.9 us -> 18.5 us
  starting transfers between devices: 22.9 us -> 19.7 us
  blocking collectives: 11.7 us -> 14.8 us
    ppermute x14 -> x12, waiting for transfers between devices: 109 us -> 67.3 us  [the longest x8 48.7 us: fetched(): return lax.ppermute(value, AXES, route)]
    pallas_call x1 -> x2, Pallas kernels: 11.9 us -> 18.5 us  [the longest x1 10.1 us: on_device(): pl.pallas_call(functools.partial(early_kernel, rows, keep), out_shape=(ja...]
    select_n x1 -> x5, other arithmetic: 0.01 us -> 3.76 us  [the longest x2 2.26 us: steps(): brought = jnp.where(z >= line - 2, brought_up, brought_down)]
    all_to_all x1, blocking collectives: 11.7 us -> 14.8 us  [on_device(): lax.all_to_all(spread_out.reshape(3, devices, rows * groups), AXES, split...]
    ppermute x14 -> x12, starting transfers between devices: 22.9 us -> 19.7 us  [the longest x8 17.1 us: fetched(): return lax.ppermute(value, AXES, route)]
    convert_element_type x0 -> x7, other arithmetic: none -> 2.67 us  [the longest x6 2.67 us: columns_of(): x[half:half + rows, :keep].astype(jnp.int32)]
    unnamed x13 -> x15, local copies, waits for them, and re-layouts: 3.62 us -> 1.02 us
  transfers between devices with their start and end apart: 14 -> 12, of which waited for: 7 -> 7; matrix products, arithmetic and copies ran while one was open for 3% -> 8% of each run, Pallas kernels for 0% -> 7%
where the time goes in v3:
time: 140 us
  waiting for transfers between devices  67.3 us (48%)
  starting transfers between devices  19.7 us (14%)
  Pallas kernels  18.5 us (13%)
  blocking collectives  14.8 us (11%)
  other arithmetic  10.3 us (7%)
  local copies, waits for them, and re-layouts  6.21 us (4%)
  matrix products  1.93 us (1%)
    ppermute x8, waiting for transfers between devices, fetched(): return lax.ppermute(value, AXES, route)  48.7 us
    ppermute x2, waiting for transfers between devices, steps(): near = lax.ppermute(brought, AXES, over + under)  18.6 us
    ppermute x8, starting transfers between devices, fetched(): return lax.ppermute(value, AXES, route)  17.1 us
    all_to_all x1, blocking collectives, on_device(): lax.all_to_all(spread_out.reshape(3, devices, rows * groups), AXES, split...  14.8 us
    pallas_call x1, Pallas kernels, on_device(): pl.pallas_call(functools.partial(early_kernel, rows, keep), out_shape=(ja...  10.1 us
    pallas_call x1, Pallas kernels, on_device(): pl.pallas_call(functools.partial(late_kernel, rows, keep), out_shape=(jax...  8.44 us
  transfers between devices with their start and end apart: 12, of which 7 were waited for; matrix products, arithmetic and copies ran while one was open for 8% of the time, Pallas kernels for 7%

profile of v3, /device:TPU:0, one launch (start us, length us, event | category | flops | bytes accessed | tf_op | source)
XLA Modules:
  0.0 139.7 jit_solution(4402196637466631888)
XLA Ops:
  0.7 1.3 add_select_fusion.4
  2.0 1.5 %fusion.12 = (bf16[2,12,128,128]{3,2,1,0:T(8,128)(2,1)S(1)}, bf16[2,12,128,128]{3,2,1,0:T(8,128)(2,1)S(1)}) fusion(bf16[4,12,128,128]{3,2,1,0:T(8,128)(2,1)} %param.5), kind=kLoop, calls=%fused_computation.51 | loop fusion | bytes 3145728 | tf_op jit(solution)/shard_map/slice | solution.py:196
  3.6 1.4 %collective-permute-start.2 = (bf16[3088,128]{1,0:T(8,128)(2,1)S(1)}, bf16[3088,128]{1,0:T(8,128)(2,1)}, u32[]{:S(2)}, u32[]{:S(2)}) collective-permute-start(bf16[3088,128]{1,0:T(8,128)(2,1)S(1)} %fusion.5), channel_id=1, source_target_pairs={{1,0},{2,1},{3,2},{5,4},{6,5},{7,6},{9,8},{10,9},{11,10},{13,12},{... | collective-permute-start | bytes 2371592 | tf_op jit(solution)/shard_map/ppermute | solution.py:19
  5.1 6.4 %collective-permute-start = (bf16[3088,128]{1,0:T(8,128)(2,1)S(1)}, bf16[3088,128]{1,0:T(8,128)(2,1)}, u32[]{:S(2)}, u32[]{:S(2)}) collective-permute-start(bf16[3088,128]{1,0:T(8,128)(2,1)S(1)} %fusion.5), channel_id=1, source_target_pairs={{0,1},{1,2},{2,3},{4,5},{5,6},{6,7},{8,9},{9,10},{10,11},{12,13},{... | collective-permute-start | bytes 2371592 | tf_op jit(solution)/shard_map/ppermute | solution.py:19
  12.4 3.9 %collective-permute-start.6 = (bf16[3104,128]{1,0:T(8,128)(2,1)}, bf16[3104,128]{1,0:T(8,128)(2,1)}, u32[]{:S(2)}, u32[]{:S(2)}) collective-permute-start(bf16[3104,128]{1,0:T(8,128)(2,1)} %pad.9), channel_id=1, source_target_pairs={{0,1},{1,2},{2,3},{4,5},{5,6},{6,7},{8,9},{9,10},{10,11},{12,13},{... | collective-permute-start | bytes 2383880 | tf_op jit(solution)/shard_map/ppermute | solution.py:19
  16.4 1.3 collective-permute-start.8
  19.9 7.4 %collective-permute-done.2.refs_4_ = bf16[3088,128]{1,0:T(8,128)(2,1)} collective-permute-done((bf16[3088,128]{1,0:T(8,128)(2,1)S(1)}, bf16[3088,128]{1,0:T(8,128)(2,1)}, u32[]{:S(2)}, u32[]{:S(2)}) %collective-permute-start.2) | collective-permute-done | bytes 790560 | tf_op jit(solution)/shard_map/ppermute | solution.py:19
  27.2 1.3 collective-permute-start.3
  29.5 1.4 copy.14
  32.2 12.4 %collective-permute-done.6.refs_1_ = bf16[3104,128]{1,0:T(8,128)(2,1)} collective-permute-done((bf16[3104,128]{1,0:T(8,128)(2,1)}, bf16[3104,128]{1,0:T(8,128)(2,1)}, u32[]{:S(2)}, u32[]{:S(2)}) %collective-permute-start.6) | collective-permute-done | bytes 794656 | tf_op jit(solution)/shard_map/ppermute | solution.py:19
  45.3 1.3 collective-permute-start.9
  46.6 14.5 %collective-permute-done.3.refs_6_ = bf16[3088,128]{1,0:T(8,128)(2,1)S(1)} collective-permute-done((bf16[3088,128]{1,0:T(8,128)(2,1)}, bf16[3088,128]{1,0:T(8,128)(2,1)S(1)}, u32[]{:S(2)}, u32[]{:S(2)}) %collective-permute-start.3) | collective-permute-done | bytes 790560 | tf_op jit(solution)/shard_map/ppermute | solution.py:19
  61.1 1.1 broadcast_select_fusion.1
  62.2 1.3 collective-permute-start.5
  63.8 14.3 %collective-permute-done.9.refs_7_ = bf16[3104,128]{1,0:T(8,128)(2,1)S(1)} collective-permute-done((bf16[3104,128]{1,0:T(8,128)(2,1)}, bf16[3104,128]{1,0:T(8,128)(2,1)S(1)}, u32[]{:S(2)}, u32[]{:S(2)}) %collective-permute-start.9) | collective-permute-done | bytes 794656 | tf_op jit(solution)/shard_map/ppermute | solution.py:19
  78.1 1.2 broadcast_select_fusion
  79.3 1.3 collective-permute-start.10
  81.4 10.1 %early.1 = (f32[4,12,128,128]{3,2,1,0:T(8,128)}, bf16[512,1024]{1,0:T(8,128)(2,1)}) custom-call(s32[20,20]{1,0:T(8,128)} %select_reduce_fusion.where_ref, s32[4,12]{1,0:T(4,128)} %get-tuple-element.10.column_ref, s32[2]{0:T(128)} %pad_add_fusion.place_ref, bf16[6144,128]{1,0:T(8,128)(2,1)} %bitcast.21, bf16[3088,128]{1,0:T(8,128)(2,1)} %collective-permute-done.refs_0_, ...), custom_call_target="tpu_custom_call" | custom-call | tf_op jit(solution)/shard_map/early/pallas_call | solution.py:253
  91.5 3.8 %collective-permute-done.5.refs_1_ = bf16[3088,128]{1,0:T(8,128)(2,1)} collective-permute-done((bf16[3088,128]{1,0:T(8,128)(2,1)}, bf16[3088,128]{1,0:T(8,128)(2,1)}, u32[]{:S(2)}, u32[]{:S(2)}) %collective-permute-start.5) | collective-permute-done | bytes 790560 | tf_op jit(solution)/shard_map/ppermute | solution.py:214
  97.4 14.9 %collective-permute-done.10.refs_2_ = bf16[3104,128]{1,0:T(8,128)(2,1)} collective-permute-done((bf16[3104,128]{1,0:T(8,128)(2,1)}, bf16[3104,128]{1,0:T(8,128)(2,1)}, u32[]{:S(2)}, u32[]{:S(2)}) %collective-permute-start.10) | collective-permute-done | bytes 794656 | tf_op jit(solution)/shard_map/ppermute | solution.py:214
  113.2 8.4 %late.1 = (bf16[4,12,128,128]{3,2,1,0:T(8,128)(2,1)}, f32[3,4,32,128]{3,2,1,0:T(8,128)}) custom-call(s32[8,16]{1,0:T(8,128)} %select_reduce_fusion.1.where_ref, s32[4,12]{1,0:T(4,128)} %get-tuple-element.10.column_ref, s32[2]{0:T(128)} %pad_add_fusion.place_ref, bf16[512,1024]{1,0:T(8,128)(2,1)} %get-tuple-element.6.refs_0_, ...), custom_call_target="tpu_custom_call" | custom-call | tf_op jit(solution)/shard_map/late/pallas_call | solution.py:273
  121.6 1.1 reduce_sum.18
  122.8 1.4 %fusion = f32[3,32,128]{2,0,1:T(4,128)S(1)} fusion(f32[3,128,1]{1,0,2:T(4,128)S(1)} %reshape.231, s32[32,128]{1,0:T(8,128)S(1)} %multiply_add_fusion, s32[128]{0:T(128)S(1)} %copy-done.6), kind=kOutput, calls=%fused_computation.1 | convolution fusion | flops 19398656 | bytes 67584 | tf_op jit(solution)/shard_map/dot_general | solution.py:298
  124.2 14.8 %all_to_all.5 = f32[3,32,128]{2,0,1:T(4,128)S(1)} all-to-all(f32[3,32,128]{2,0,1:T(4,128)S(1)} %fusion), channel_id=1, replica_groups=mesh['layer'=2,'row'=4,'col'=4] {'layer','row','col'}, dimensions={1} | all-to-all | bytes 98304 | tf_op jit(solution)/shard_map/all_to_all | solution.py:299
  (58 shorter events, 11.0 us)
Async XLA Ops:
  3.6 14.1 %copy-start.5 = (bf16[3,4,12,1024]{3,1,2,0:T(4,128)(2,1)S(1)}, bf16[3,4,12,1024]{3,1,2,0:T(4,128)(2,1)}, u32[]{:S(2)}) copy-start(bf16[3,4,12,1024]{3,1,2,0:T(4,128)(2,1)} %param.8) | copy-start | bytes 884740
  3.6 23.6 %collective-permute-start.2 = (bf16[3088,128]{1,0:T(8,128)(2,1)S(1)}, bf16[3088,128]{1,0:T(8,128)(2,1)}, u32[]{:S(2)}, u32[]{:S(2)}) collective-permute-start(bf16[3088,128]{1,0:T(8,128)(2,1)S(1)} %fusion.5), channel_id=1, source_target_pairs={{1,0},{2,1},{3,2},{5,4},{6,5},{7,6},{9,8},{10,9},{11,10},{13,12},{... | collective-permute-start | bytes 2371592 | tf_op jit(solution)/shard_map/ppermute | solution.py:19
  5.1 23.6 %collective-permute-start = (bf16[3088,128]{1,0:T(8,128)(2,1)S(1)}, bf16[3088,128]{1,0:T(8,128)(2,1)}, u32[]{:S(2)}, u32[]{:S(2)}) collective-permute-start(bf16[3088,128]{1,0:T(8,128)(2,1)S(1)} %fusion.5), channel_id=1, source_target_pairs={{0,1},{1,2},{2,3},{4,5},{5,6},{6,7},{8,9},{9,10},{10,11},{12,13},{... | collective-permute-start | bytes 2371592 | tf_op jit(solution)/shard_map/ppermute | solution.py:19
  12.4 32.2 %collective-permute-start.6 = (bf16[3104,128]{1,0:T(8,128)(2,1)}, bf16[3104,128]{1,0:T(8,128)(2,1)}, u32[]{:S(2)}, u32[]{:S(2)}) collective-permute-start(bf16[3104,128]{1,0:T(8,128)(2,1)} %pad.9), channel_id=1, source_target_pairs={{0,1},{1,2},{2,3},{4,5},{5,6},{6,7},{8,9},{9,10},{10,11},{12,13},{... | collective-permute-start | bytes 2383880 | tf_op jit(solution)/shard_map/ppermute | solution.py:19
  16.4 29.0 %collective-permute-start.8 = (bf16[3104,128]{1,0:T(8,128)(2,1)}, bf16[3104,128]{1,0:T(8,128)(2,1)}, u32[]{:S(2)}, u32[]{:S(2)}) collective-permute-start(bf16[3104,128]{1,0:T(8,128)(2,1)} %pad.9), channel_id=1, source_target_pairs={{1,0},{2,1},{3,2},{5,4},{6,5},{7,6},{9,8},{10,9},{11,10},{13,12},{... | collective-permute-start | bytes 2383880 | tf_op jit(solution)/shard_map/ppermute | solution.py:19
  27.2 33.9 %collective-permute-start.3 = (bf16[3088,128]{1,0:T(8,128)(2,1)}, bf16[3088,128]{1,0:T(8,128)(2,1)S(1)}, u32[]{:S(2)}, u32[]{:S(2)}) collective-permute-start(bf16[3088,128]{1,0:T(8,128)(2,1)} %collective-permute-done.2.refs_4_), channel_id=1, source_target_pairs={{1,0},{2,1},{5,4},{6,5},{9,8},{10,9},{13,12},{14,13},{17,16},{18,1... | collective-permute-start | bytes 2371592 | tf_op jit(solution)/shard_map/ppermute | solution.py:19
  28.6 32.5 %collective-permute-start.1 = (bf16[3088,128]{1,0:T(8,128)(2,1)}, bf16[3088,128]{1,0:T(8,128)(2,1)S(1)}, u32[]{:S(2)}, u32[]{:S(2)}) collective-permute-start(bf16[3088,128]{1,0:T(8,128)(2,1)} %collective-permute-done.refs_0_), channel_id=1, source_target_pairs={{1,2},{2,3},{5,6},{6,7},{9,10},{10,11},{13,14},{14,15},{17,18},{18... | collective-permute-start | bytes 2371592 | tf_op jit(solution)/shard_map/ppermute | solution.py:19
  44.6 19.2 %collective-permute-start.7 = (bf16[3104,128]{1,0:T(8,128)(2,1)}, bf16[3104,128]{1,0:T(8,128)(2,1)S(1)}, u32[]{:S(2)}, u32[]{:S(2)}) collective-permute-start(bf16[3104,128]{1,0:T(8,128)(2,1)} %collective-permute-done.6.refs_1_), channel_id=1, source_target_pairs={{1,2},{2,3},{5,6},{6,7},{9,10},{10,11},{13,14},{14,15},{17,18},{18... | collective-permute-start | bytes 2383880 | tf_op jit(solution)/shard_map/ppermute | solution.py:19
  45.3 32.8 %collective-permute-start.9 = (bf16[3104,128]{1,0:T(8,128)(2,1)}, bf16[3104,128]{1,0:T(8,128)(2,1)S(1)}, u32[]{:S(2)}, u32[]{:S(2)}) collective-permute-start(bf16[3104,128]{1,0:T(8,128)(2,1)} %collective-permute-done.8.refs_5_), channel_id=1, source_target_pairs={{1,0},{2,1},{5,4},{6,5},{9,8},{10,9},{13,12},{14,13},{17,16},{18,1... | collective-permute-start | bytes 2383880 | tf_op jit(solution)/shard_map/ppermute | solution.py:19
  61.1 18.2 %copy-start.2 = (bf16[3088,128]{1,0:T(8,128)(2,1)}, bf16[3088,128]{1,0:T(8,128)(2,1)S(1)}, u32[]{:S(2)}) copy-start(bf16[3088,128]{1,0:T(8,128)(2,1)S(1)} %collective-permute-done.3.refs_6_) | copy-start | bytes 2371588
  61.1 18.2 %copy-start.3 = (bf16[3088,128]{1,0:T(8,128)(2,1)}, bf16[3088,128]{1,0:T(8,128)(2,1)S(1)}, u32[]{:S(2)}) copy-start(bf16[3088,128]{1,0:T(8,128)(2,1)S(1)} %collective-permute-done.1.refs_2_) | copy-start | bytes 2371588
  62.2 33.0 %collective-permute-start.5 = (bf16[3088,128]{1,0:T(8,128)(2,1)}, bf16[3088,128]{1,0:T(8,128)(2,1)}, u32[]{:S(2)}, u32[]{:S(2)}) collective-permute-start(bf16[3088,128]{1,0:T(8,128)(2,1)} %broadcast_select_fusion.1), channel_id=1, source_target_pairs={{6,3},{10,7},{14,11},{18,15},{22,19},{26,23},{30,27},{2,31},{29,0}... | collective-permute-start | bytes 2371592 | tf_op jit(solution)/shard_map/ppermute | solution.py:214
  63.5 32.4 %collective-permute-start.4 = (bf16[3088,128]{1,0:T(8,128)(2,1)}, bf16[3088,128]{1,0:T(8,128)(2,1)}, u32[]{:S(2)}, u32[]{:S(2)}) collective-permute-start(bf16[3088,128]{1,0:T(8,128)(2,1)} %broadcast_select_fusion.1), channel_id=1, source_target_pairs={{6,2},{7,3},{10,6},{11,7},{14,10},{15,11},{18,14},{19,15},{22,18},... | collective-permute-start | bytes 2371592 | tf_op jit(solution)/shard_map/ppermute | solution.py:217
  63.8 17.6 %copy-start = (bf16[3104,128]{1,0:T(8,128)(2,1)}, bf16[3104,128]{1,0:T(8,128)(2,1)S(1)}, u32[]{:S(2)}) copy-start(bf16[3104,128]{1,0:T(8,128)(2,1)S(1)} %collective-permute-done.7.refs_3_) | copy-start | bytes 2383876
  78.1 3.3 %copy-start.1 = (bf16[3104,128]{1,0:T(8,128)(2,1)}, bf16[3104,128]{1,0:T(8,128)(2,1)S(1)}, u32[]{:S(2)}) copy-start(bf16[3104,128]{1,0:T(8,128)(2,1)S(1)} %collective-permute-done.9.refs_7_) | copy-start | bytes 2383876
  79.3 33.0 %collective-permute-start.10 = (bf16[3104,128]{1,0:T(8,128)(2,1)}, bf16[3104,128]{1,0:T(8,128)(2,1)}, u32[]{:S(2)}, u32[]{:S(2)}) collective-permute-start(bf16[3104,128]{1,0:T(8,128)(2,1)} %broadcast_select_fusion), channel_id=1, source_target_pairs={{6,3},{10,7},{14,11},{18,15},{22,19},{26,23},{30,27},{2,31},{29,0}... | collective-permute-start | bytes 2383880 | tf_op jit(solution)/shard_map/ppermute | solution.py:214
  80.6 31.7 %collective-permute-start.11 = (bf16[3104,128]{1,0:T(8,128)(2,1)}, bf16[3104,128]{1,0:T(8,128)(2,1)S(1)}, u32[]{:S(2)}, u32[]{:S(2)}) collective-permute-start(bf16[3104,128]{1,0:T(8,128)(2,1)} %broadcast_select_fusion), channel_id=1, source_target_pairs={{6,2},{7,3},{10,6},{11,7},{14,10},{15,11},{18,14},{19,15},{22,18},... | collective-permute-start | bytes 2383880 | tf_op jit(solution)/shard_map/ppermute | solution.py:217
  112.3 0.9 copy-start.4
  113.2 9.6 %copy-start.6 = (s32[128]{0:T(128)S(1)}, s32[128]{0:T(128)}, u32[]{:S(2)}) copy-start(s32[128]{0:T(128)} %param.9) | copy-start | bytes 1540

commit v4 on v3

--- a/solution.py
+++ b/solution.py
@@ -17,6 +17,28 @@
     line = lax.axis_size("col")
     route = [((i + offset) % total, i) for i in range(total) if keep(i % line)]
     return lax.ppermute(value, AXES, route)
+
+
+def pack_kernel(rows, blocks, pattern_ref, flat, first, second, wide, sems):
+    half = flat.shape[0] // 2
+    position = lax.axis_index(AXES)
+    copies = [
+        pltpu.make_async_copy(flat.at[pl.ds(n * half, half)], part.at[pl.ds(0, half)], sems.at[n])
+        for n, part in enumerate((first, second))
+    ]
+    for copy in copies:
+        copy.start()
+    pattern = pattern_ref[...]
+    reach = 2 * rows
+    row = position * rows + lax.broadcasted_iota(jnp.int32, pattern.shape, 0)
+    distance = lax.rem(pattern - row + (reach + blocks), blocks) - reach
+    distance = jnp.where(pattern >= 0, distance, UNUSED)
+    wide[...] = jnp.zeros_like(wide)
+    wide[: pattern.shape[0], : pattern.shape[1]] = distance.astype(jnp.float32)
+    first[pl.ds(half, TAIL)] = wide[...].astype(first.dtype)
+    second[pl.ds(half, 2 * TAIL)] = jnp.zeros((2 * TAIL, second.shape[1]), second.dtype)
+    for copy in copies:
+        copy.wait()
 
 
 def early_kernel(rows, keep, where_ref, column_ref, place_ref, own, *refs):
@@ -67,9 +89,12 @@
                 block = held[pl.ds(2 * height + (i * keep + l) * size, size)]
                 left[i * size : (i + 1) * size, pl.ds(at, size)] = block
 
-    width = late_ref.shape[1]
-    start = pl.multiple_of(jnp.where(z <= 1, 0, span * size - width), size)
-    late_ref[...] = left[:, pl.ds(start, width)]
+    width = late_ref.shape[2] // 2
+    start = jnp.where(z <= 1, 0, span * size - 4 * width)
+    for h in range(2):
+        for part in range(2):
+            at = pl.multiple_of(start + (2 * part + h) * width, size)
+            late_ref[h, :, part * width : (part + 1) * width] = left[:, pl.ds(at, width)]
     put_left = pltpu.make_async_copy(late_ref, late_out, out_sems.at[rows])
     put_left.start()
     for part, pair, valid in sources:
@@ -96,7 +121,7 @@
     put_mixture = []
     for i in range(rows):
 
-        @pl.loop(0, keep)
+        @pl.loop(0, keep, unroll=True)
         def _(k, i=i):
             column = column_ref[i, k]
             term = square[jnp.maximum(column, 0), i * size : (i + 1) * size, :]
@@ -111,52 +136,89 @@
         put.wait()
 
 
-def late_kernel(rows, keep, where_ref, column_ref, place_ref, *refs):
-    left_in, near_a, near_b, far_a, far_b, mixture_in, ham_in, factor_in, next_out, force_ref = refs[:10]
-    left, held, mixture_ref, ham_ref, factor_ref, next_ref, square, product, sems, out_sems = refs[10:]
+def late_terms(rows, keep, half, where_ref, place_ref, given, left, held, square, sems):
+    left_in, near, far = given
+    size = held.shape[1]
+    reach = 2 * rows
+    count = reach * keep * size // 4
+    low = place_ref[0] <= 1
+    near_at = pl.multiple_of(jnp.where(low, count, 0), size)
+    far_at = pl.multiple_of(jnp.where(low, 0, count), size)
+    gets = [
+        pltpu.make_async_copy(far.at[pl.ds(0, count)], held.at[pl.ds(far_at, count)], sems.at[1]),
+        pltpu.make_async_copy(near.at[pl.ds(0, count)], held.at[pl.ds(near_at, count)], sems.at[2]),
+    ]
+    if left_in is not None:
+        gets.append(pltpu.make_async_copy(left_in.at[half], left, sems.at[0]))
+    for get in gets:
+        get.start()
+    held[pl.ds(2 * count, size)] = jnp.zeros((size, size), held.dtype)
+
+    def block(r, c):
+        return held[pl.ds(pl.multiple_of(where_ref[r, c] * size, size), size)]
+
+    def finish():
+        for get in gets:
+            get.wait()
+        span = [part * rows + half * rows // 2 + n for part in range(2) for n in range(rows // 2)]
+        for j in range(0, 2 * reach, 2):
+            right = jnp.concatenate(
+                [jnp.concatenate([block(r, j), block(r, j + 1)], axis=1) for r in span], axis=0
+            )
+            total = jnp.dot(left[...], right, preferred_element_type=jnp.float32)
+            square[j] = total[:, :size]
+            square[j + 1] = total[:, size:]
+
+    def term(column, i):
+        place = column - jnp.where(low, 0, rows)
+        inside = (column >= 0) & (place >= 0) & (place < 2 * reach)
+        value = square[jnp.where(inside, place, 0), i * size : (i + 1) * size, :]
+        return jnp.where(inside, value, 0.0)
+
+    return finish, term
+
+
+def middle_kernel(
+    rows, keep, where_ref, column_ref, place_ref, left_in, near, far, mixture_in, ham_in, factor_in, mine_in,
+    mixture_ref, ham, factor, mine, left_out,
+    left, held, square, sems, row_sems,
+):
+    given = (left_in, near, far)
+    finish, term = late_terms(rows, keep, 0, where_ref, place_ref, given, left, held, square, sems)
+    gets = [pltpu.make_async_copy(mixture_in.at[i], mixture_ref.at[i], row_sems.at[i]) for i in range(rows)]
+    kept = [(ham_in, ham), (factor_in, factor), (mine_in, mine), (left_in.at[1], left_out)]
+    others = [
+        pltpu.make_async_copy(there, here, row_sems.at[rows + n]) for n, (there, here) in enumerate(kept)
+    ]
+    for get in gets + others:
+        get.start()
+    finish()
+    for i in range(rows):
+        gets[i].wait()
+
+        @pl.loop(0, keep, unroll=True)
+        def _(k, i=i):
+            mixture_ref[i, k] = mixture_ref[i, k] - term(column_ref[i, k], i)
+
+    for get in others:
+        get.wait()
+
+
+def late_kernel(
+    rows, keep, where_ref, column_ref, place_ref, near, far, mixture_ref, ham_ref, factor_ref, mine, left,
+    next_out, force_ref,
+    held, next_ref, square, product, sums_ref, sems, out_sems,
+):
+    given = (None, near, far)
+    finish, term = late_terms(rows, keep, 1, where_ref, place_ref, given, left, held, square, sems)
     size = ham_ref.shape[2]
     groups = size // 4
-    span = 5 * rows
-    reach = 2 * rows
-    height = rows * keep * size
-    half = height // 2
-    low = place_ref[0] <= 1
-    near_at = pl.multiple_of(jnp.where(low, height, 0), size)
-    far_at = pl.multiple_of(jnp.where(low, 0, height), size)
-    routes = [(left_in, left)]
-    for there, at in ((far_a, far_at), (near_a, near_at), (far_b, far_at + half), (near_b, near_at + half)):
-        routes.append((there.at[pl.ds(0, half)], held.at[pl.ds(pl.multiple_of(at, size), half)]))
-    routes += [(mixture_in, mixture_ref), (ham_in, ham_ref), (factor_in, factor_ref)]
-    gets = [pltpu.make_async_copy(there, here, sems.at[n]) for n, (there, here) in enumerate(routes)]
-    for get in gets:
-        get.start()
-    held[pl.ds(2 * height, size)] = jnp.zeros((size, size), held.dtype)
-    for get in gets[:5]:
-        get.wait()
-
-    def block(r, c):
-        return held[pl.ds(pl.multiple_of(where_ref[r, c] * size, size), size)]
-
-    for j in range(0, 2 * reach, 2):
-        right = jnp.concatenate(
-            [jnp.concatenate([block(r, j), block(r, j + 1)], axis=1) for r in range(reach)], axis=0
-        )
-        total = jnp.dot(left[...], right, preferred_element_type=jnp.float32)
-        square[j] = total[:, :size]
-        square[j + 1] = total[:, size:]
-
-    for get in gets[5:]:
-        get.wait()
-    offset = jnp.where(low, 0, span - 2 * reach)
-    puts = []
+    puts = [pltpu.make_async_copy(next_ref.at[i], next_out.at[i], out_sems.at[i]) for i in range(rows)]
+    finish()
     for i in range(rows):
 
         def slot(k, sums, i=i):
-            column = column_ref[i, k]
-            place = column - offset
-            inside = (column >= 0) & (place >= 0) & (place < 2 * reach)
-            term = square[jnp.where(inside, place, 0), i * size : (i + 1) * size, :]
-            mixture = mixture_ref[i, k] - jnp.where(inside, term, 0.0)
+            mixture = mixture_ref[i, k] - term(column_ref[i, k], i)
             next_ref[i, k] = mixture.astype(next_ref.dtype)
             product[...] = mixture * ham_ref[i, k].astype(jnp.float32)
             energy = product[pl.ds(0, groups, stride=4), :]
@@ -165,13 +227,42 @@
             return tuple(sums[d] + energy * factor_ref[d, i, k].astype(jnp.float32) for d in range(3))
 
         start = tuple(jnp.zeros((groups, size), jnp.float32) for _ in range(3))
-        sums = lax.fori_loop(0, keep, slot, start)
-        puts.append(pltpu.make_async_copy(next_ref.at[i], next_out.at[i], out_sems.at[i]))
+        sums = lax.fori_loop(0, keep, slot, start, unroll=True)
         puts[i].start()
         for d in range(3):
-            force_ref[d, i] = sums[d]
+            sums_ref[d, i * groups : (i + 1) * groups] = sums[d]
+
+    def split(value):
+        high = value.astype(jnp.bfloat16)
+        rest = value - high.astype(jnp.float32)
+        middle = rest.astype(jnp.bfloat16)
+        low = (rest - middle.astype(jnp.float32)).astype(jnp.bfloat16)
+        return high, middle, low
+
+    ones = jnp.ones((8, size), jnp.bfloat16)
+    line = lax.broadcasted_iota(jnp.int32, (8, rows * groups), 0)
+    force = jnp.zeros((8, rows * groups), jnp.float32)
+    for d in range(3):
+        total = sum(
+            lax.dot_general(ones, part, (((1,), (1,)), ((), ())), preferred_element_type=jnp.float32)
+            for part in split(sums_ref[d])
+        )
+        force = jnp.where(line == d, total, force)
+    parts = jnp.concatenate([part.astype(jnp.float32) for part in split(force)], axis=0).astype(jnp.bfloat16)
+    own_atoms = force_ref.shape[2]
+    batch = 8
     for put in puts:
         put.wait()
+
+    def place(n, carry):
+        at = pl.multiple_of(n * batch * own_atoms, own_atoms)
+        placed = jnp.dot(parts, mine[:, pl.ds(at, batch * own_atoms)], preferred_element_type=jnp.float32)
+        placed = placed[:8] + placed[8:16] + placed[16:]
+        for e in range(batch):
+            force_ref[n * batch + e] = placed[:3, e * own_atoms : (e + 1) * own_atoms]
+        return carry
+
+    lax.fori_loop(0, force_ref.shape[0] // batch, place, 0, unroll=True if force_ref.shape[0] <= 64 else 1)
 
 
 def on_device(density, pattern, ham_derivative, pair_direction, atom_of_group):
@@ -189,11 +280,17 @@
     row_at = jnp.arange(span, dtype=jnp.int32)[:, None]
     distance = jnp.mod(pattern - (position * rows + row_at[:rows]) + reach, blocks) - reach
     distance = jnp.where(pattern >= 0, distance, UNUSED)
-    tail = jnp.pad(distance.astype(jnp.bfloat16), ((0, TAIL - rows), (0, size - keep)))
-
     flat = density.reshape(rows * keep * size, size)
     half = rows * keep * size // 2
-    parts = [jnp.concatenate([flat[:half], tail], axis=0), jnp.pad(flat[half:], ((0, 2 * TAIL), (0, 0)))]
+    parts = pl.pallas_call(
+        functools.partial(pack_kernel, rows, blocks),
+        out_shape=[pltpu.VMEM((half + n, size), density.dtype) for n in (TAIL, 2 * TAIL)],
+        in_specs=[pl.BlockSpec(memory_space=pltpu.VMEM), pl.BlockSpec(memory_space=pltpu.HBM)],
+        out_specs=[pl.BlockSpec(memory_space=pltpu.VMEM)] * 2,
+        scratch_shapes=[pltpu.VMEM((TAIL, size), jnp.float32), pltpu.SemaphoreType.DMA((2,))],
+        compiler_params=pltpu.CompilerParams(vmem_limit_bytes=56 * 1024 * 1024),
+        name="pack",
+    )(pattern, flat)
 
     def columns_of(pieces):
         return jnp.concatenate([x[half : half + rows, :keep].astype(jnp.int32) for x in pieces], axis=0)
@@ -239,7 +336,10 @@
     first = jnp.where(low, 0, reach)
     late = jnp.where(known & (late != UNUSED), late + first + row_at[:reach], -1)
     hit = late[:, :, None] == jnp.arange(2 * reach, dtype=jnp.int32)[None, None, :]
-    where_late = jnp.min(jnp.where(hit, flat_slot[:reach], reach * keep), axis=1)
+    at = row_at[:reach]
+    local = at // rows * (rows // 2) + at % (rows // 2)
+    late_slot = local[:, :, None] * keep + jnp.arange(keep, dtype=jnp.int32)[None, :, None]
+    where_late = jnp.min(jnp.where(hit, late_slot, rows * keep), axis=1)
     place = jnp.stack([z, jnp.int32(line)]).astype(jnp.int32)
 
     spread = jnp.repeat(jnp.eye(groups, dtype=jnp.bfloat16), 4, axis=1)
@@ -250,11 +350,13 @@
     vmem = pl.BlockSpec(memory_space=pltpu.VMEM)
     smem = pl.BlockSpec(memory_space=pltpu.SMEM)
     limit = pltpu.CompilerParams(vmem_limit_bytes=60 * 1024 * 1024)
+    mine = (atom_of_group[:, None] == jnp.arange(atoms, dtype=jnp.int32)[None, :]).astype(jnp.bfloat16)
+    where_early, factor, mine = lax.optimization_barrier((where_early, factor, mine))
     mixture, left = pl.pallas_call(
         functools.partial(early_kernel, rows, keep),
         out_shape=(
             jax.ShapeDtypeStruct(density.shape, jnp.float32),
-            jax.ShapeDtypeStruct((rows * size, reach * size), jnp.bfloat16),
+            jax.ShapeDtypeStruct((2, rows * size, rows * size), jnp.bfloat16),
         ),
         in_specs=[smem] * 3 + [hbm] * 9,
         out_specs=(hbm, hbm),
@@ -263,43 +365,54 @@
             pltpu.VMEM((rows * size, span * size), jnp.bfloat16),
             pltpu.VMEM((span, rows * size, size), jnp.float32),
             pltpu.VMEM(density.shape, jnp.float32),
-            pltpu.VMEM((rows * size, reach * size), jnp.bfloat16),
+            pltpu.VMEM((2, rows * size, rows * size), jnp.bfloat16),
             pltpu.SemaphoreType.DMA((5, 2)),
             pltpu.SemaphoreType.DMA((rows + 1,)),
         ],
         compiler_params=limit,
         name="early",
     )(where_early, columns, place, flat, *[x for pair in zip(line_a, line_b) for x in pair])
-    next_density, sums = pl.pallas_call(
+    held_shape = ((rows * keep + 1) * size, size)
+    square_shape = (2 * reach, rows * size, size)
+    kept = [mixture, ham_derivative, factor, mine, left[1]]
+    room = 60 * 1024 * 1024 - sum(x.size * x.dtype.itemsize for x in kept)
+    kept = pl.pallas_call(
+        functools.partial(middle_kernel, rows, keep),
+        out_shape=[pltpu.VMEM(x.shape, x.dtype) for x in kept],
+        in_specs=[smem] * 3 + [hbm] * 7,
+        out_specs=[vmem] * 5,
+        scratch_shapes=[
+            pltpu.VMEM(left.shape[1:], left.dtype),
+            pltpu.VMEM(held_shape, jnp.bfloat16),
+            pltpu.VMEM(square_shape, jnp.float32),
+            pltpu.SemaphoreType.DMA((3,)),
+            pltpu.SemaphoreType.DMA((rows + 4,)),
+        ],
+        compiler_params=pltpu.CompilerParams(vmem_limit_bytes=room),
+        name="middle",
+    )(where_late, columns, place, left, near_a, far_a, mixture, ham_derivative, factor, mine)
+    next_density, pieces = pl.pallas_call(
         functools.partial(late_kernel, rows, keep),
         out_shape=(
             jax.ShapeDtypeStruct(density.shape, density.dtype),
-            jax.ShapeDtypeStruct((3, rows, groups, size), jnp.float32),
+            jax.ShapeDtypeStruct((devices, 3, rows * groups), jnp.float32),
         ),
-        in_specs=[smem] * 3 + [hbm] * 8,
+        in_specs=[smem] * 3 + [hbm] * 2 + [vmem] * 5,
         out_specs=(hbm, vmem),
         scratch_shapes=[
-            pltpu.VMEM(left.shape, left.dtype),
-            pltpu.VMEM(((reach * keep + 1) * size, size), jnp.bfloat16),
-            pltpu.VMEM(mixture.shape, mixture.dtype),
-            pltpu.VMEM(ham_derivative.shape, ham_derivative.dtype),
-            pltpu.VMEM(factor.shape, factor.dtype),
+            pltpu.VMEM(held_shape, jnp.bfloat16),
             pltpu.VMEM(density.shape, density.dtype),
-            pltpu.VMEM((2 * reach, rows * size, size), jnp.float32),
+            pltpu.VMEM(square_shape, jnp.float32),
             pltpu.VMEM((size, size), jnp.float32),
-            pltpu.SemaphoreType.DMA((8,)),
+            pltpu.VMEM((3, rows * groups, size), jnp.float32),
+            pltpu.SemaphoreType.DMA((3,)),
             pltpu.SemaphoreType.DMA((rows,)),
         ],
-        compiler_params=limit,
+        compiler_params=pltpu.CompilerParams(vmem_limit_bytes=32 * 1024 * 1024),
         name="late",
-    )(where_late, columns, place, left, near_a, near_b, far_a, far_b, mixture, ham_derivative, factor)
-    force = jnp.sum(sums, axis=3).reshape(3, rows * groups)
-    mine = (atom_of_group[:, None] == jnp.arange(atoms, dtype=jnp.int32)[None, :]).astype(jnp.float32)
-    spread_out = jnp.dot(force, mine, precision=lax.Precision.HIGHEST)
-    pieces = lax.all_to_all(
-        spread_out.reshape(3, devices, rows * groups), AXES, split_axis=1, concat_axis=1, tiled=True
-    )
-    return next_density, jnp.sum(pieces, axis=1)
+    )(where_late, columns, place, near_b, far_b, *kept)
+    pieces = lax.all_to_all(pieces, AXES, split_axis=0, concat_axis=0, tiled=True)
+    return next_density, jnp.sum(pieces, axis=0)
 
 
 def solution(mesh):

time: 140 us -> 131 us (0.936)
  waiting for transfers between devices: 67.3 us -> 54.3 us
  Pallas kernels: 18.5 us -> 22.5 us
  local copies, waits for them, and re-layouts: 6.21 us -> 3.7 us
  other arithmetic: 10.3 us -> 11.8 us
  starting transfers between devices: 19.7 us -> 21.1 us
    pallas_call x0 -> x2, Pallas kernels: none -> 8.4 us  [the longest x1 6.26 us: on_device(): pl.pallas_call(functools.partial(middle_kernel, rows, keep), out_shape=[p...]
    ppermute x8, waiting for transfers between devices: 48.7 us -> 42 us  [fetched(): return lax.ppermute(value, AXES, route)]
    ppermute x2, waiting for transfers between devices: 18.6 us -> 12.4 us  [steps(): near = lax.ppermute(brought, AXES, over + under)]
    pallas_call x1, Pallas kernels: 8.44 us -> 4.13 us  [on_device(): pl.pallas_call(functools.partial(late_kernel, rows, keep), out_shape=(jax...]
    slice x1 -> x0, local copies, waits for them, and re-layouts: 1.54 us -> none  [on_device(): flat[half:]]
    dot_general x1 -> x0, matrix products: 1.45 us -> none  [on_device(): spread_out = jnp.dot(force, mine, precision=lax.Precision.HIGHEST)]
  transfers between devices with their start and end apart: 12 -> 12, of which waited for: 7 -> 7; matrix products, arithmetic and copies ran while one was open for 8% -> 13% of each run, Pallas kernels for 7% -> 12%
where the time goes in v4:
time: 131 us
  waiting for transfers between devices  54.3 us (41%)
  Pallas kernels  22.5 us (17%)
  starting transfers between devices  21.1 us (16%)
  blocking collectives  14.8 us (11%)
  other arithmetic  11.8 us (9%)
  local copies, waits for them, and re-layouts  3.7 us (3%)
  matrix products  1.75 us (1%)
    ppermute x8, waiting for transfers between devices, fetched(): return lax.ppermute(value, AXES, route)  42 us
    ppermute x8, starting transfers between devices, fetched(): return lax.ppermute(value, AXES, route)  18.4 us
    all_to_all x1, blocking collectives, on_device(): lax.all_to_all(pieces, AXES, split_axis=0, concat_axis=0, tiled=True)  14.8 us
    ppermute x2, waiting for transfers between devices, steps(): near = lax.ppermute(brought, AXES, over + under)  12.4 us
    pallas_call x1, Pallas kernels, on_device(): pl.pallas_call(functools.partial(early_kernel, rows, keep), out_shape=(ja...  9.98 us
    pallas_call x1, Pallas kernels, on_device(): pl.pallas_call(functools.partial(middle_kernel, rows, keep), out_shape=[p...  6.26 us
    pallas_call x1, Pallas kernels, on_device(): pl.pallas_call(functools.partial(late_kernel, rows, keep), out_shape=(jax...  4.13 us
    select_n x2, other arithmetic, steps(): brought = jnp.where(z >= line - 2, brought_up, brought_down)  3.64 us
  transfers between devices with their start and end apart: 12, of which 7 were waited for; matrix products, arithmetic and copies ran while one was open for 13% of the time, Pallas kernels for 12%

profile of v4, /device:TPU:0, one launch (start us, length us, event | category | flops | bytes accessed | tf_op | source)
XLA Modules:
  0.0 130.8 jit_solution(12858601843533696760)
XLA Ops:
  0.6 2.1 %pack.1 = (bf16[3088,128]{1,0:T(8,128)(2,1)S(1)}, bf16[3104,128]{1,0:T(8,128)(2,1)S(1)}) custom-call(s32[4,12]{1,0:T(4,128)} %pattern_ref.1, bf16[6144,128]{1,0:T(8,128)(2,1)} %bitcast.18), custom_call_target="tpu_custom_call" | custom-call | tf_op jit(solution)/shard_map/pack/pallas_call | solution.py:285
  2.8 1.3 collective-permute-start.2
  4.1 6.4 %collective-permute-start = (bf16[3088,128]{1,0:T(8,128)(2,1)S(1)}, bf16[3088,128]{1,0:T(8,128)(2,1)}, u32[]{:S(2)}, u32[]{:S(2)}) collective-permute-start(bf16[3088,128]{1,0:T(8,128)(2,1)S(1)} %get-tuple-element.16), channel_id=1, source_target_pairs={{0,1},{1,2},{2,3},{4,5},{5,6},{6,7},{8,9},{9,10},{10,11},{12,13},{... | collective-permute-start | bytes 2371592 | tf_op jit(solution)/shard_map/ppermute | solution.py:19
  10.5 1.3 collective-permute-start.8
  11.8 5.5 %collective-permute-start.6 = (bf16[3104,128]{1,0:T(8,128)(2,1)S(1)}, bf16[3104,128]{1,0:T(8,128)(2,1)}, u32[]{:S(2)}, u32[]{:S(2)}) collective-permute-start(bf16[3104,128]{1,0:T(8,128)(2,1)S(1)} %get-tuple-element.17), channel_id=1, source_target_pairs={{0,1},{1,2},{2,3},{4,5},{5,6},{6,7},{8,9},{9,10},{10,11},{12,13},{... | collective-permute-start | bytes 2383880 | tf_op jit(solution)/shard_map/ppermute | solution.py:19
  17.4 1.9 %reshape.221 = bf16[4608,32]{1,0:T(8,128)(2,1)} reshape(bf16[3,4,12,1024]{3,2,1,0:T(8,128)(2,1)S(1)} %copy.12) | data formatting | bytes 589824 | tf_op jit(solution)/shard_map/reshape | solution.py:346
  20.1 1.8 %convolution_bitcast_fusion = bf16[4608,128]{0,1:T(8,128)(2,1)S(1)} fusion(bf16[32,128]{0,1:T(8,128)(2,1)S(1)} %bitcast.21, bf16[4608,32]{1,0:T(8,128)(2,1)} %reshape.221), kind=kOutput, calls=%fused_computation | convolution fusion | flops 37748736 | bytes 1482752 | tf_op jit(solution)/shard_map/dot_general | solution.py:346
  21.8 1.3 fusion.mine_in
  23.1 3.2 %collective-permute-done.2.refs_4_ = bf16[3088,128]{1,0:T(8,128)(2,1)} collective-permute-done((bf16[3088,128]{1,0:T(8,128)(2,1)S(1)}, bf16[3088,128]{1,0:T(8,128)(2,1)}, u32[]{:S(2)}, u32[]{:S(2)}) %collective-permute-start.2) | collective-permute-done | bytes 790560 | tf_op jit(solution)/shard_map/ppermute | solution.py:19
  26.3 1.3 collective-permute-start.3
  29.0 1.4 %copy.13 = bf16[4608,128]{1,0:T(8,128)(2,1)} copy(bf16[4608,128]{0,1:T(8,128)(2,1)S(1)} %convolution_bitcast_fusion) | data formatting | bytes 2359296 | tf_op jit(solution)/shard_map/dot_general | solution.py:346
  31.8 11.6 %collective-permute-done.8.refs_5_ = bf16[3104,128]{1,0:T(8,128)(2,1)} collective-permute-done((bf16[3104,128]{1,0:T(8,128)(2,1)S(1)}, bf16[3104,128]{1,0:T(8,128)(2,1)}, u32[]{:S(2)}, u32[]{:S(2)}) %collective-permute-start.8) | collective-permute-done | bytes 794656 | tf_op jit(solution)/shard_map/ppermute | solution.py:19
  43.3 1.3 collective-permute-start.9
  45.3 14.9 %collective-permute-done.3.refs_6_ = bf16[3088,128]{1,0:T(8,128)(2,1)} collective-permute-done((bf16[3088,128]{1,0:T(8,128)(2,1)}, bf16[3088,128]{1,0:T(8,128)(2,1)}, u32[]{:S(2)}, u32[]{:S(2)}) %collective-permute-start.3) | collective-permute-done | bytes 790560 | tf_op jit(solution)/shard_map/ppermute | solution.py:19
  60.3 2.5 %broadcast_select_fusion.1 = bf16[3088,128]{1,0:T(8,128)(2,1)} fusion(bf16[3088,128]{1,0:T(8,128)(2,1)S(1)} %collective-permute-done.1.refs_2_, bf16[3088,128]{1,0:T(8,128)(2,1)} %collective-permute-done.3.refs_6_, pred[]{:T(512)S(6)} %ge.15), kind=kLoop, calls=%fused_computation.4 | loop fusion | flops 395264 | bytes 2371585 | tf_op jit(solution)/shard_map/jit(_where)/select_n | solution.py:307
  62.7 1.3 collective-permute-start.5
  65.0 12.2 %collective-permute-done.9.refs_7_ = bf16[3104,128]{1,0:T(8,128)(2,1)S(1)} collective-permute-done((bf16[3104,128]{1,0:T(8,128)(2,1)}, bf16[3104,128]{1,0:T(8,128)(2,1)S(1)}, u32[]{:S(2)}, u32[]{:S(2)}) %collective-permute-start.9) | collective-permute-done | bytes 794656 | tf_op jit(solution)/shard_map/ppermute | solution.py:19
  78.4 1.3 collective-permute-start.10
  80.4 10.0 %early.1 = (f32[4,12,128,128]{3,2,1,0:T(8,128)}, bf16[2,512,512]{2,1,0:T(8,128)(2,1)}) custom-call(s32[20,20]{1,0:T(8,128)} %select_reduce_fusion.where_ref, s32[4,12]{1,0:T(4,128)} %get-tuple-element.30.column_ref, s32[2]{0:T(128)} %pad_add_fusion.place_ref, bf16[6144,128]{1,0:T(8,128)(2,1)} %bitcast.19, bf16[3088,128]{1,0:T(8,128)(2,1)} %collective-permute-done.refs_0_, ...), custom_call_target="tpu_custom_call" | custom-call | tf_op jit(solution)/shard_map/early/pallas_call | solution.py:355
  90.4 3.9 %collective-permute-done.5.near = bf16[3088,128]{1,0:T(8,128)(2,1)} collective-permute-done((bf16[3088,128]{1,0:T(8,128)(2,1)}, bf16[3088,128]{1,0:T(8,128)(2,1)}, u32[]{:S(2)}, u32[]{:S(2)}) %collective-permute-start.5) | collective-permute-done | bytes 790560 | tf_op jit(solution)/shard_map/ppermute | solution.py:311
  96.4 6.3 %middle.1 = (f32[4,12,128,128]{3,2,1,0:T(8,128)S(1)}, bf16[4,12,128,128]{3,2,1,0:T(8,128)(2,1)S(1)}, bf16[3,4,12,32,128]{4,3,2,1,0:T(8,128)(2,1)S(1)}, bf16[128,4096]{1,0:T(8,128)(2,1)S(1)}, bf16[512,512]{1,0:T(8,128)(2,1)S(1)}) custom-call(s32[8,16]{1,0:T(8,128)} %select_reduce_fusion.1.where_ref, s32[4,12]{1,0:T(4,128)} %get-tuple-element.30.column_ref, ...), custom_call_target="tpu_custom_call" | custom-call | tf_op jit(solution)/shard_map/middle/pallas_call | solution.py:379
  102.7 8.5 %collective-permute-done.10.near = bf16[3104,128]{1,0:T(8,128)(2,1)S(1)} collective-permute-done((bf16[3104,128]{1,0:T(8,128)(2,1)}, bf16[3104,128]{1,0:T(8,128)(2,1)S(1)}, u32[]{:S(2)}, u32[]{:S(2)}) %collective-permute-start.10) | collective-permute-done | bytes 794656 | tf_op jit(solution)/shard_map/ppermute | solution.py:311
  111.2 4.1 %late.1 = (bf16[4,12,128,128]{3,2,1,0:T(8,128)(2,1)}, f32[32,3,128]{2,1,0:T(4,128)S(1)}) custom-call(s32[8,16]{1,0:T(8,128)S(1)} %copy-done, s32[4,12]{1,0:T(4,128)S(1)} %copy-done.1, s32[2]{0:T(128)S(1)} %copy-done.2, bf16[3104,128]{1,0:T(8,128)(2,1)S(1)} %collective-permute-done.10.near, bf16[3104,128]{1,0:T(8,128)(2,1)S(1)} %collective-permute-done.11.far, ...), custom_call_target="tpu_custom_call" | custom-call | tf_op jit(solution)/shard_map/late/pallas_call | solution.py:394
  115.3 14.8 %all_to_all.5 = f32[32,3,128]{2,1,0:T(4,128)S(1)} all-to-all(f32[32,3,128]{2,1,0:T(4,128)S(1)} %get-tuple-element.29), channel_id=1, replica_groups=mesh['layer'=2,'row'=4,'col'=4] {'layer','row','col'}, dimensions={0} | all-to-all | bytes 98304 | tf_op jit(solution)/shard_map/all_to_all | solution.py:414
  (56 shorter events, 10.0 us)
Async XLA Ops:
  0.6 16.7 %copy-start.6 = (bf16[3,4,12,1024]{3,1,2,0:T(4,128)(2,1)S(1)}, bf16[3,4,12,1024]{3,1,2,0:T(4,128)(2,1)}, u32[]{:S(2)}) copy-start(bf16[3,4,12,1024]{3,1,2,0:T(4,128)(2,1)} %param.8) | copy-start | bytes 884740
  0.6 18.8 %copy-start.7 = (s32[4,12]{1,0:T(4,128)S(1)}, s32[4,12]{1,0:T(4,128)}, u32[]{:S(2)}) copy-start(s32[4,12]{1,0:T(4,128)} %pattern_ref.1) | copy-start | bytes 580
  2.8 23.5 %collective-permute-start.2 = (bf16[3088,128]{1,0:T(8,128)(2,1)S(1)}, bf16[3088,128]{1,0:T(8,128)(2,1)}, u32[]{:S(2)}, u32[]{:S(2)}) collective-permute-start(bf16[3088,128]{1,0:T(8,128)(2,1)S(1)} %get-tuple-element.16), channel_id=1, source_target_pairs={{1,0},{2,1},{3,2},{5,4},{6,5},{7,6},{9,8},{10,9},{11,10},{13,12},{... | collective-permute-start | bytes 2371592 | tf_op jit(solution)/shard_map/ppermute | solution.py:19
  4.1 23.6 %collective-permute-start = (bf16[3088,128]{1,0:T(8,128)(2,1)S(1)}, bf16[3088,128]{1,0:T(8,128)(2,1)}, u32[]{:S(2)}, u32[]{:S(2)}) collective-permute-start(bf16[3088,128]{1,0:T(8,128)(2,1)S(1)} %get-tuple-element.16), channel_id=1, source_target_pairs={{0,1},{1,2},{2,3},{4,5},{5,6},{6,7},{8,9},{9,10},{10,11},{12,13},{... | collective-permute-start | bytes 2371592 | tf_op jit(solution)/shard_map/ppermute | solution.py:19
  10.5 32.8 %collective-permute-start.8 = (bf16[3104,128]{1,0:T(8,128)(2,1)S(1)}, bf16[3104,128]{1,0:T(8,128)(2,1)}, u32[]{:S(2)}, u32[]{:S(2)}) collective-permute-start(bf16[3104,128]{1,0:T(8,128)(2,1)S(1)} %get-tuple-element.17), channel_id=1, source_target_pairs={{1,0},{2,1},{3,2},{5,4},{6,5},{7,6},{9,8},{10,9},{11,10},{13,12},{... | collective-permute-start | bytes 2383880 | tf_op jit(solution)/shard_map/ppermute | solution.py:19
  11.8 32.8 %collective-permute-start.6 = (bf16[3104,128]{1,0:T(8,128)(2,1)S(1)}, bf16[3104,128]{1,0:T(8,128)(2,1)}, u32[]{:S(2)}, u32[]{:S(2)}) collective-permute-start(bf16[3104,128]{1,0:T(8,128)(2,1)S(1)} %get-tuple-element.17), channel_id=1, source_target_pairs={{0,1},{1,2},{2,3},{4,5},{5,6},{6,7},{8,9},{9,10},{10,11},{12,13},{... | collective-permute-start | bytes 2383880 | tf_op jit(solution)/shard_map/ppermute | solution.py:19
  19.3 2.5 %copy-start.8 = (s32[128]{0:T(128)S(1)}, s32[128]{0:T(128)}, u32[]{:S(2)}) copy-start(s32[128]{0:T(128)} %param.9) | copy-start | bytes 1540
  26.3 34.0 %collective-permute-start.3 = (bf16[3088,128]{1,0:T(8,128)(2,1)}, bf16[3088,128]{1,0:T(8,128)(2,1)}, u32[]{:S(2)}, u32[]{:S(2)}) collective-permute-start(bf16[3088,128]{1,0:T(8,128)(2,1)} %collective-permute-done.2.refs_4_), channel_id=1, source_target_pairs={{1,0},{2,1},{5,4},{6,5},{9,8},{10,9},{13,12},{14,13},{17,16},{18,1... | collective-permute-start | bytes 2371592 | tf_op jit(solution)/shard_map/ppermute | solution.py:19
  27.7 32.6 %collective-permute-start.1 = (bf16[3088,128]{1,0:T(8,128)(2,1)}, bf16[3088,128]{1,0:T(8,128)(2,1)S(1)}, u32[]{:S(2)}, u32[]{:S(2)}) collective-permute-start(bf16[3088,128]{1,0:T(8,128)(2,1)} %collective-permute-done.refs_0_), channel_id=1, source_target_pairs={{1,2},{2,3},{5,6},{6,7},{9,10},{10,11},{13,14},{14,15},{17,18},{18... | collective-permute-start | bytes 2371592 | tf_op jit(solution)/shard_map/ppermute | solution.py:19
  43.3 33.9 %collective-permute-start.9 = (bf16[3104,128]{1,0:T(8,128)(2,1)}, bf16[3104,128]{1,0:T(8,128)(2,1)S(1)}, u32[]{:S(2)}, u32[]{:S(2)}) collective-permute-start(bf16[3104,128]{1,0:T(8,128)(2,1)} %collective-permute-done.8.refs_5_), channel_id=1, source_target_pairs={{1,0},{2,1},{5,4},{6,5},{9,8},{10,9},{13,12},{14,13},{17,16},{18,1... | collective-permute-start | bytes 2383880 | tf_op jit(solution)/shard_map/ppermute | solution.py:19
  44.6 32.6 %collective-permute-start.7 = (bf16[3104,128]{1,0:T(8,128)(2,1)}, bf16[3104,128]{1,0:T(8,128)(2,1)S(1)}, u32[]{:S(2)}, u32[]{:S(2)}) collective-permute-start(bf16[3104,128]{1,0:T(8,128)(2,1)} %collective-permute-done.6.refs_1_), channel_id=1, source_target_pairs={{1,2},{2,3},{5,6},{6,7},{9,10},{10,11},{13,14},{14,15},{17,18},{18... | collective-permute-start | bytes 2383880 | tf_op jit(solution)/shard_map/ppermute | solution.py:19
  60.3 18.1 %copy-start.5 = (bf16[3088,128]{1,0:T(8,128)(2,1)}, bf16[3088,128]{1,0:T(8,128)(2,1)S(1)}, u32[]{:S(2)}) copy-start(bf16[3088,128]{1,0:T(8,128)(2,1)S(1)} %collective-permute-done.1.refs_2_) | copy-start | bytes 2371588
  62.7 31.5 %collective-permute-start.5 = (bf16[3088,128]{1,0:T(8,128)(2,1)}, bf16[3088,128]{1,0:T(8,128)(2,1)}, u32[]{:S(2)}, u32[]{:S(2)}) collective-permute-start(bf16[3088,128]{1,0:T(8,128)(2,1)} %broadcast_select_fusion.1), channel_id=1, source_target_pairs={{6,3},{10,7},{14,11},{18,15},{22,19},{26,23},{30,27},{2,31},{29,0}... | collective-permute-start | bytes 2371592 | tf_op jit(solution)/shard_map/ppermute | solution.py:311
  64.0 30.9 %collective-permute-start.4 = (bf16[3088,128]{1,0:T(8,128)(2,1)}, bf16[3088,128]{1,0:T(8,128)(2,1)}, u32[]{:S(2)}, u32[]{:S(2)}) collective-permute-start(bf16[3088,128]{1,0:T(8,128)(2,1)} %broadcast_select_fusion.1), channel_id=1, source_target_pairs={{6,2},{7,3},{10,6},{11,7},{14,10},{15,11},{18,14},{19,15},{22,18},... | collective-permute-start | bytes 2371592 | tf_op jit(solution)/shard_map/ppermute | solution.py:314
  77.2 3.2 %copy-start.3 = (bf16[3104,128]{1,0:T(8,128)(2,1)}, bf16[3104,128]{1,0:T(8,128)(2,1)S(1)}, u32[]{:S(2)}) copy-start(bf16[3104,128]{1,0:T(8,128)(2,1)S(1)} %collective-permute-done.9.refs_7_) | copy-start | bytes 2383876
  77.2 3.2 %copy-start.4 = (bf16[3104,128]{1,0:T(8,128)(2,1)}, bf16[3104,128]{1,0:T(8,128)(2,1)S(1)}, u32[]{:S(2)}) copy-start(bf16[3104,128]{1,0:T(8,128)(2,1)S(1)} %collective-permute-done.7.refs_3_) | copy-start | bytes 2383876
  78.3 24.4 %collective-permute-start.11 = (bf16[3104,128]{1,0:T(8,128)(2,1)}, bf16[3104,128]{1,0:T(8,128)(2,1)S(1)}, u32[]{:S(2)}, u32[]{:S(2)}) collective-permute-start(bf16[3104,128]{1,0:T(8,128)(2,1)} %broadcast_select_fusion), channel_id=1, source_target_pairs={{6,2},{7,3},{10,6},{11,7},{14,10},{15,11},{18,14},{19,15},{22,18},... | collective-permute-start | bytes 2383880 | tf_op jit(solution)/shard_map/ppermute | solution.py:314
  78.4 32.8 %collective-permute-start.10 = (bf16[3104,128]{1,0:T(8,128)(2,1)}, bf16[3104,128]{1,0:T(8,128)(2,1)S(1)}, u32[]{:S(2)}, u32[]{:S(2)}) collective-permute-start(bf16[3104,128]{1,0:T(8,128)(2,1)} %broadcast_select_fusion), channel_id=1, source_target_pairs={{6,3},{10,7},{14,11},{18,15},{22,19},{26,23},{30,27},{2,31},{29,0}... | collective-permute-start | bytes 2383880 | tf_op jit(solution)/shard_map/ppermute | solution.py:311
  96.4 14.8 %copy-start = (s32[8,16]{1,0:T(8,128)S(1)}, s32[8,16]{1,0:T(8,128)}, u32[]{:S(2)}) copy-start(s32[8,16]{1,0:T(8,128)} %select_reduce_fusion.1.where_ref) | copy-start | bytes 1540
  96.4 14.8 %copy-start.1 = (s32[4,12]{1,0:T(4,128)S(1)}, s32[4,12]{1,0:T(4,128)}, u32[]{:S(2)}) copy-start(s32[4,12]{1,0:T(4,128)} %get-tuple-element.30.column_ref) | copy-start | bytes 580
  96.4 14.8 %copy-start.2 = (s32[2]{0:T(128)S(1)}, s32[2]{0:T(128)}, u32[]{:S(2)}) copy-start(s32[2]{0:T(128)} %pad_add_fusion.place_ref) | copy-start | bytes 28

commit v5 on v4

--- a/solution.py
+++ b/solution.py
@@ -220,14 +220,17 @@
         def slot(k, sums, i=i):
             mixture = mixture_ref[i, k] - term(column_ref[i, k], i)
             next_ref[i, k] = mixture.astype(next_ref.dtype)
-            product[...] = mixture * ham_ref[i, k].astype(jnp.float32)
-            energy = product[pl.ds(0, groups, stride=4), :]
+            spot = product.at[k % 4]
+            spot[...] = mixture * ham_ref[i, k].astype(jnp.float32)
+            energy = spot[pl.ds(0, groups, stride=4), :]
             for r in range(1, 4):
-                energy = energy + product[pl.ds(r, groups, stride=4), :]
+                energy = energy + spot[pl.ds(r, groups, stride=4), :]
             return tuple(sums[d] + energy * factor_ref[d, i, k].astype(jnp.float32) for d in range(3))
 
         start = tuple(jnp.zeros((groups, size), jnp.float32) for _ in range(3))
-        sums = lax.fori_loop(0, keep, slot, start, unroll=True)
+        sums = start
+        for k in range(keep):
+            sums = slot(k, sums)
         puts[i].start()
         for d in range(3):
             sums_ref[d, i * groups : (i + 1) * groups] = sums[d]
@@ -251,8 +254,6 @@
     parts = jnp.concatenate([part.astype(jnp.float32) for part in split(force)], axis=0).astype(jnp.bfloat16)
     own_atoms = force_ref.shape[2]
     batch = 8
-    for put in puts:
-        put.wait()
 
     def place(n, carry):
         at = pl.multiple_of(n * batch * own_atoms, own_atoms)
@@ -263,6 +264,8 @@
         return carry
 
     lax.fori_loop(0, force_ref.shape[0] // batch, place, 0, unroll=True if force_ref.shape[0] <= 64 else 1)
+    for put in puts:
+        put.wait()
 
 
 def on_device(density, pattern, ham_derivative, pair_direction, atom_of_group):
@@ -305,6 +308,7 @@
             brought_up = fetched(brought_up, -1, lambda z: z >= step)
             brought_down = fetched(brought_down, 1, lambda z: z <= line - 1 - step)
         brought = jnp.where(z >= line - 2, brought_up, brought_down)
+        brought = brought[: half + TAIL] if part is parts[0] else brought[:half]
         total = line * lax.axis_size(("layer", "row"))
         over = [((i + line - 1) % total, i) for i in range(total) if i % line == line - 1]
         under = [((i + 1 - line) % total, i) for i in range(total) if i % line == 0]
@@ -403,7 +407,7 @@
             pltpu.VMEM(held_shape, jnp.bfloat16),
             pltpu.VMEM(density.shape, density.dtype),
             pltpu.VMEM(square_shape, jnp.float32),
-            pltpu.VMEM((size, size), jnp.float32),
+            pltpu.VMEM((4, size, size), jnp.float32),
             pltpu.VMEM((3, rows * groups, size), jnp.float32),
             pltpu.SemaphoreType.DMA((3,)),
             pltpu.SemaphoreType.DMA((rows,)),

time: 131 us -> 131 us (level)
  waiting for transfers between devices: 54.3 us -> 52.9 us
    select_n x2, other arithmetic: 3.64 us -> 2.06 us  [steps(): brought = jnp.where(z >= line - 2, brought_up, brought_down)]
where the time goes in v5:
time: 131 us; the launch traced here: 130 us
  waiting for transfers between devices  52.9 us (40%)
  Pallas kernels  22.2 us (17%)
  starting transfers between devices  21.2 us (16%)
  blocking collectives  14.8 us (11%)
  other arithmetic  11.9 us (9%)
  local copies, waits for them, and re-layouts  4.66 us (4%)
  matrix products  1.75 us (1%)
    ppermute x8, waiting for transfers between devices, fetched(): return lax.ppermute(value, AXES, route)  40.8 us
    ppermute x8, starting transfers between devices, fetched(): return lax.ppermute(value, AXES, route)  18.6 us
    all_to_all x1, blocking collectives, on_device(): lax.all_to_all(pieces, AXES, split_axis=0, concat_axis=0, tiled=True)  14.8 us
    ppermute x2, waiting for transfers between devices, steps(): near = lax.ppermute(brought, AXES, over + under)  12.1 us
    pallas_call x1, Pallas kernels, on_device(): pl.pallas_call(functools.partial(early_kernel, rows, keep), out_shape=(ja...  9.97 us
    pallas_call x1, Pallas kernels, on_device(): pl.pallas_call(functools.partial(middle_kernel, rows, keep), out_shape=[p...  6.26 us
    pallas_call x1, Pallas kernels, on_device(): pl.pallas_call(functools.partial(late_kernel, rows, keep), out_shape=(jax...  3.79 us
    convert_element_type x6, other arithmetic, columns_of(): x[half:half + rows, :keep].astype(jnp.int32)  2.71 us
  transfers between devices with their start and end apart: 12, of which 7 were waited for; matrix products, arithmetic and copies ran while one was open for 13% of the time, Pallas kernels for 12%

profile of v5, /device:TPU:0, one launch (start us, length us, event | category | flops | bytes accessed | tf_op | source)
XLA Modules:
  0.0 130.3 jit_solution(1696599241692554758)
XLA Ops:
  0.6 2.1 %pack.1 = (bf16[3088,128]{1,0:T(8,128)(2,1)S(1)}, bf16[3104,128]{1,0:T(8,128)(2,1)S(1)}) custom-call(s32[4,12]{1,0:T(4,128)} %pattern_ref.1, bf16[6144,128]{1,0:T(8,128)(2,1)} %bitcast.18), custom_call_target="tpu_custom_call" | custom-call | tf_op jit(solution)/shard_map/pack/pallas_call | solution.py:288
  2.8 1.3 collective-permute-start.2
  4.1 6.5 %collective-permute-start = (bf16[3088,128]{1,0:T(8,128)(2,1)S(1)}, bf16[3088,128]{1,0:T(8,128)(2,1)}, u32[]{:S(2)}, u32[]{:S(2)}) collective-permute-start(bf16[3088,128]{1,0:T(8,128)(2,1)S(1)} %get-tuple-element.16), channel_id=1, source_target_pairs={{0,1},{1,2},{2,3},{4,5},{5,6},{6,7},{8,9},{9,10},{10,11},{12,13},{... | collective-permute-start | bytes 2371592 | tf_op jit(solution)/shard_map/ppermute | solution.py:19
  10.6 1.3 collective-permute-start.8
  11.9 5.5 %collective-permute-start.6 = (bf16[3104,128]{1,0:T(8,128)(2,1)S(1)}, bf16[3104,128]{1,0:T(8,128)(2,1)}, u32[]{:S(2)}, u32[]{:S(2)}) collective-permute-start(bf16[3104,128]{1,0:T(8,128)(2,1)S(1)} %get-tuple-element.17), channel_id=1, source_target_pairs={{0,1},{1,2},{2,3},{4,5},{5,6},{6,7},{8,9},{9,10},{10,11},{12,13},{... | collective-permute-start | bytes 2383880 | tf_op jit(solution)/shard_map/ppermute | solution.py:19
  18.7 1.9 %reshape.221 = bf16[4608,32]{1,0:T(8,128)(2,1)} reshape(bf16[3,4,12,1024]{3,2,1,0:T(8,128)(2,1)S(1)} %copy.12) | data formatting | bytes 589824 | tf_op jit(solution)/shard_map/reshape | solution.py:350
  21.9 1.8 %convolution_bitcast_fusion = bf16[4608,128]{0,1:T(8,128)(2,1)S(1)} fusion(bf16[32,128]{0,1:T(8,128)(2,1)S(1)} %bitcast.21, bf16[4608,32]{1,0:T(8,128)(2,1)} %reshape.221), kind=kOutput, calls=%fused_computation | convolution fusion | flops 37748736 | bytes 1482752 | tf_op jit(solution)/shard_map/dot_general | solution.py:350
  23.7 1.2 fusion.mine_in
  24.9 1.4 %collective-permute-done.2.refs_4_ = bf16[3088,128]{1,0:T(8,128)(2,1)} collective-permute-done((bf16[3088,128]{1,0:T(8,128)(2,1)S(1)}, bf16[3088,128]{1,0:T(8,128)(2,1)}, u32[]{:S(2)}, u32[]{:S(2)}) %collective-permute-start.2) | collective-permute-done | bytes 790560 | tf_op jit(solution)/shard_map/ppermute | solution.py:19
  26.3 1.3 collective-permute-start.3
  29.0 1.4 %copy.13 = bf16[4608,128]{1,0:T(8,128)(2,1)} copy(bf16[4608,128]{0,1:T(8,128)(2,1)S(1)} %convolution_bitcast_fusion) | data formatting | bytes 2359296 | tf_op jit(solution)/shard_map/dot_general | solution.py:350
  32.4 10.9 %collective-permute-done.8.refs_5_ = bf16[3104,128]{1,0:T(8,128)(2,1)} collective-permute-done((bf16[3104,128]{1,0:T(8,128)(2,1)S(1)}, bf16[3104,128]{1,0:T(8,128)(2,1)}, u32[]{:S(2)}, u32[]{:S(2)}) %collective-permute-start.8) | collective-permute-done | bytes 794656 | tf_op jit(solution)/shard_map/ppermute | solution.py:19
  43.3 1.3 collective-permute-start.9
  45.3 14.8 %collective-permute-done.3.refs_6_ = bf16[3088,128]{1,0:T(8,128)(2,1)S(1)} collective-permute-done((bf16[3088,128]{1,0:T(8,128)(2,1)}, bf16[3088,128]{1,0:T(8,128)(2,1)S(1)}, u32[]{:S(2)}, u32[]{:S(2)}) %collective-permute-start.3) | collective-permute-done | bytes 790560 | tf_op jit(solution)/shard_map/ppermute | solution.py:19
  60.1 1.1 broadcast_select_fusion
  61.2 1.3 collective-permute-start.5
  63.6 13.6 %collective-permute-done.9.refs_7_ = bf16[3104,128]{1,0:T(8,128)(2,1)S(1)} collective-permute-done((bf16[3104,128]{1,0:T(8,128)(2,1)}, bf16[3104,128]{1,0:T(8,128)(2,1)S(1)}, u32[]{:S(2)}, u32[]{:S(2)}) %collective-permute-start.9) | collective-permute-done | bytes 794656 | tf_op jit(solution)/shard_map/ppermute | solution.py:19
  79.1 1.3 collective-permute-start.10
  80.5 10.0 %early.1 = (f32[4,12,128,128]{3,2,1,0:T(8,128)}, bf16[2,512,512]{2,1,0:T(8,128)(2,1)}) custom-call(s32[20,20]{1,0:T(8,128)} %select_reduce_fusion.where_ref, s32[4,12]{1,0:T(4,128)} %get-tuple-element.30.column_ref, s32[2]{0:T(128)} %pad_add_fusion.place_ref, bf16[6144,128]{1,0:T(8,128)(2,1)} %bitcast.19, bf16[3088,128]{1,0:T(8,128)(2,1)} %collective-permute-done.refs_0_, ...), custom_call_target="tpu_custom_call" | custom-call | tf_op jit(solution)/shard_map/early/pallas_call | solution.py:359
  90.5 3.8 %collective-permute-done.5.near = bf16[3088,128]{1,0:T(8,128)(2,1)} collective-permute-done((bf16[3088,128]{1,0:T(8,128)(2,1)}, bf16[3088,128]{1,0:T(8,128)(2,1)}, u32[]{:S(2)}, u32[]{:S(2)}) %collective-permute-start.5) | collective-permute-done | bytes 790560 | tf_op jit(solution)/shard_map/ppermute | solution.py:315
  96.5 6.3 %middle.1 = (f32[4,12,128,128]{3,2,1,0:T(8,128)S(1)}, bf16[4,12,128,128]{3,2,1,0:T(8,128)(2,1)S(1)}, bf16[3,4,12,32,128]{4,3,2,1,0:T(8,128)(2,1)S(1)}, bf16[128,4096]{1,0:T(8,128)(2,1)S(1)}, bf16[512,512]{1,0:T(8,128)(2,1)S(1)}) custom-call(s32[8,16]{1,0:T(8,128)} %select_reduce_fusion.1.where_ref, s32[4,12]{1,0:T(4,128)} %get-tuple-element.30.column_ref, ...), custom_call_target="tpu_custom_call" | custom-call | tf_op jit(solution)/shard_map/middle/pallas_call | solution.py:383
  102.8 8.3 %collective-permute-done.10.near = bf16[3072,128]{1,0:T(8,128)(2,1)S(1)} collective-permute-done((bf16[3072,128]{1,0:T(8,128)(2,1)}, bf16[3072,128]{1,0:T(8,128)(2,1)S(1)}, u32[]{:S(2)}, u32[]{:S(2)}) %collective-permute-start.10) | collective-permute-done | bytes 786464 | tf_op jit(solution)/shard_map/ppermute | solution.py:315
  111.0 3.8 %late.1 = (bf16[4,12,128,128]{3,2,1,0:T(8,128)(2,1)}, f32[32,3,128]{2,1,0:T(4,128)S(1)}) custom-call(s32[8,16]{1,0:T(8,128)S(1)} %copy-done, s32[4,12]{1,0:T(4,128)S(1)} %copy-done.1, s32[2]{0:T(128)S(1)} %copy-done.2, bf16[3072,128]{1,0:T(8,128)(2,1)S(1)} %collective-permute-done.10.near, bf16[3072,128]{1,0:T(8,128)(2,1)S(1)} %collective-permute-done.11.far, ...), custom_call_target="tpu_custom_call" | custom-call | tf_op jit(solution)/shard_map/late/pallas_call | solution.py:398
  114.8 14.8 %all_to_all.5 = f32[32,3,128]{2,1,0:T(4,128)S(1)} all-to-all(f32[32,3,128]{2,1,0:T(4,128)S(1)} %get-tuple-element.29), channel_id=1, replica_groups=mesh['layer'=2,'row'=4,'col'=4] {'layer','row','col'}, dimensions={0} | all-to-all | bytes 98304 | tf_op jit(solution)/shard_map/all_to_all | solution.py:418
  (66 shorter events, 12.6 us)
Async XLA Ops:
  0.6 18.0 %copy-start.7 = (bf16[3,4,12,1024]{3,1,2,0:T(4,128)(2,1)S(1)}, bf16[3,4,12,1024]{3,1,2,0:T(4,128)(2,1)}, u32[]{:S(2)}) copy-start(bf16[3,4,12,1024]{3,1,2,0:T(4,128)(2,1)} %param.8) | copy-start | bytes 884740
  0.6 20.6 %copy-start.8 = (s32[4,12]{1,0:T(4,128)S(1)}, s32[4,12]{1,0:T(4,128)}, u32[]{:S(2)}) copy-start(s32[4,12]{1,0:T(4,128)} %pattern_ref.1) | copy-start | bytes 580
  2.8 23.5 %collective-permute-start.2 = (bf16[3088,128]{1,0:T(8,128)(2,1)S(1)}, bf16[3088,128]{1,0:T(8,128)(2,1)}, u32[]{:S(2)}, u32[]{:S(2)}) collective-permute-start(bf16[3088,128]{1,0:T(8,128)(2,1)S(1)} %get-tuple-element.16), channel_id=1, source_target_pairs={{1,0},{2,1},{3,2},{5,4},{6,5},{7,6},{9,8},{10,9},{11,10},{13,12},{... | collective-permute-start | bytes 2371592 | tf_op jit(solution)/shard_map/ppermute | solution.py:19
  4.1 23.6 %collective-permute-start = (bf16[3088,128]{1,0:T(8,128)(2,1)S(1)}, bf16[3088,128]{1,0:T(8,128)(2,1)}, u32[]{:S(2)}, u32[]{:S(2)}) collective-permute-start(bf16[3088,128]{1,0:T(8,128)(2,1)S(1)} %get-tuple-element.16), channel_id=1, source_target_pairs={{0,1},{1,2},{2,3},{4,5},{5,6},{6,7},{8,9},{9,10},{10,11},{12,13},{... | collective-permute-start | bytes 2371592 | tf_op jit(solution)/shard_map/ppermute | solution.py:19
  10.6 32.7 %collective-permute-start.8 = (bf16[3104,128]{1,0:T(8,128)(2,1)S(1)}, bf16[3104,128]{1,0:T(8,128)(2,1)}, u32[]{:S(2)}, u32[]{:S(2)}) collective-permute-start(bf16[3104,128]{1,0:T(8,128)(2,1)S(1)} %get-tuple-element.17), channel_id=1, source_target_pairs={{1,0},{2,1},{3,2},{5,4},{6,5},{7,6},{9,8},{10,9},{11,10},{13,12},{... | collective-permute-start | bytes 2383880 | tf_op jit(solution)/shard_map/ppermute | solution.py:19
  11.9 32.7 %collective-permute-start.6 = (bf16[3104,128]{1,0:T(8,128)(2,1)S(1)}, bf16[3104,128]{1,0:T(8,128)(2,1)}, u32[]{:S(2)}, u32[]{:S(2)}) collective-permute-start(bf16[3104,128]{1,0:T(8,128)(2,1)S(1)} %get-tuple-element.17), channel_id=1, source_target_pairs={{0,1},{1,2},{2,3},{4,5},{5,6},{6,7},{8,9},{9,10},{10,11},{12,13},{... | collective-permute-start | bytes 2383880 | tf_op jit(solution)/shard_map/ppermute | solution.py:19
  26.3 33.9 %collective-permute-start.3 = (bf16[3088,128]{1,0:T(8,128)(2,1)}, bf16[3088,128]{1,0:T(8,128)(2,1)S(1)}, u32[]{:S(2)}, u32[]{:S(2)}) collective-permute-start(bf16[3088,128]{1,0:T(8,128)(2,1)} %collective-permute-done.2.refs_4_), channel_id=1, source_target_pairs={{1,0},{2,1},{5,4},{6,5},{9,8},{10,9},{13,12},{14,13},{17,16},{18,1... | collective-permute-start | bytes 2371592 | tf_op jit(solution)/shard_map/ppermute | solution.py:19
  27.7 32.5 %collective-permute-start.1 = (bf16[3088,128]{1,0:T(8,128)(2,1)}, bf16[3088,128]{1,0:T(8,128)(2,1)S(1)}, u32[]{:S(2)}, u32[]{:S(2)}) collective-permute-start(bf16[3088,128]{1,0:T(8,128)(2,1)} %collective-permute-done.refs_0_), channel_id=1, source_target_pairs={{1,2},{2,3},{5,6},{6,7},{9,10},{10,11},{13,14},{14,15},{17,18},{18... | collective-permute-start | bytes 2371592 | tf_op jit(solution)/shard_map/ppermute | solution.py:19
  30.4 32.2 %copy-start.9 = (s32[4,12]{1,0:T(4,128)S(1)}, s32[4,12]{1,0:T(4,128)}, u32[]{:S(2)}) copy-start(s32[4,12]{1,0:T(4,128)} %get-tuple-element.31) | copy-start | bytes 580
  30.4 32.3 %copy-start.11 = (pred[20]{0:T(512)(128)(4,1)S(1)}, pred[20]{0:T(512)(128)(4,1)}, u32[]{:S(2)}) copy-start(pred[20]{0:T(512)(128)(4,1)} %or_and_fusion) | copy-start | bytes 64
  43.3 33.9 %collective-permute-start.9 = (bf16[3104,128]{1,0:T(8,128)(2,1)}, bf16[3104,128]{1,0:T(8,128)(2,1)S(1)}, u32[]{:S(2)}, u32[]{:S(2)}) collective-permute-start(bf16[3104,128]{1,0:T(8,128)(2,1)} %collective-permute-done.8.refs_5_), channel_id=1, source_target_pairs={{1,0},{2,1},{5,4},{6,5},{9,8},{10,9},{13,12},{14,13},{17,16},{18,1... | collective-permute-start | bytes 2383880 | tf_op jit(solution)/shard_map/ppermute | solution.py:19
  44.6 32.6 %collective-permute-start.7 = (bf16[3104,128]{1,0:T(8,128)(2,1)}, bf16[3104,128]{1,0:T(8,128)(2,1)S(1)}, u32[]{:S(2)}, u32[]{:S(2)}) collective-permute-start(bf16[3104,128]{1,0:T(8,128)(2,1)} %collective-permute-done.6.refs_1_), channel_id=1, source_target_pairs={{1,2},{2,3},{5,6},{6,7},{9,10},{10,11},{13,14},{14,15},{17,18},{18... | collective-permute-start | bytes 2383880 | tf_op jit(solution)/shard_map/ppermute | solution.py:19
  60.1 19.0 %copy-start.3 = (bf16[3088,128]{1,0:T(8,128)(2,1)}, bf16[3088,128]{1,0:T(8,128)(2,1)S(1)}, u32[]{:S(2)}) copy-start(bf16[3088,128]{1,0:T(8,128)(2,1)S(1)} %collective-permute-done.3.refs_6_) | copy-start | bytes 2371588
  60.1 19.0 %copy-start.4 = (bf16[3088,128]{1,0:T(8,128)(2,1)}, bf16[3088,128]{1,0:T(8,128)(2,1)S(1)}, u32[]{:S(2)}) copy-start(bf16[3088,128]{1,0:T(8,128)(2,1)S(1)} %collective-permute-done.1.refs_2_) | copy-start | bytes 2371588
  61.2 33.0 %collective-permute-start.5 = (bf16[3088,128]{1,0:T(8,128)(2,1)}, bf16[3088,128]{1,0:T(8,128)(2,1)}, u32[]{:S(2)}, u32[]{:S(2)}) collective-permute-start(bf16[3088,128]{1,0:T(8,128)(2,1)} %broadcast_select_fusion), channel_id=1, source_target_pairs={{6,3},{10,7},{14,11},{18,15},{22,19},{26,23},{30,27},{2,31},{29,0}... | collective-permute-start | bytes 2371592 | tf_op jit(solution)/shard_map/ppermute | solution.py:315
  62.5 32.4 %collective-permute-start.4 = (bf16[3088,128]{1,0:T(8,128)(2,1)}, bf16[3088,128]{1,0:T(8,128)(2,1)}, u32[]{:S(2)}, u32[]{:S(2)}) collective-permute-start(bf16[3088,128]{1,0:T(8,128)(2,1)} %broadcast_select_fusion), channel_id=1, source_target_pairs={{6,2},{7,3},{10,6},{11,7},{14,10},{15,11},{18,14},{19,15},{22,18},... | collective-permute-start | bytes 2371592 | tf_op jit(solution)/shard_map/ppermute | solution.py:318
  77.2 3.3 %copy-start.5 = (bf16[3104,128]{1,0:T(8,128)(2,1)}, bf16[3104,128]{1,0:T(8,128)(2,1)S(1)}, u32[]{:S(2)}) copy-start(bf16[3104,128]{1,0:T(8,128)(2,1)S(1)} %collective-permute-done.9.refs_7_) | copy-start | bytes 2383876
  79.1 31.9 %collective-permute-start.10 = (bf16[3072,128]{1,0:T(8,128)(2,1)}, bf16[3072,128]{1,0:T(8,128)(2,1)S(1)}, u32[]{:S(2)}, u32[]{:S(2)}) collective-permute-start(bf16[3072,128]{1,0:T(8,128)(2,1)} %slice_select_fusion), channel_id=1, source_target_pairs={{6,3},{10,7},{14,11},{18,15},{22,19},{26,23},{30,27},{2,31},{29,0}... | collective-permute-start | bytes 2359304 | tf_op jit(solution)/shard_map/ppermute | solution.py:315
  80.4 30.6 %collective-permute-start.11 = (bf16[3072,128]{1,0:T(8,128)(2,1)}, bf16[3072,128]{1,0:T(8,128)(2,1)S(1)}, u32[]{:S(2)}, u32[]{:S(2)}) collective-permute-start(bf16[3072,128]{1,0:T(8,128)(2,1)} %slice_select_fusion), channel_id=1, source_target_pairs={{6,2},{7,3},{10,6},{11,7},{14,10},{15,11},{18,14},{19,15},{22,18},... | collective-permute-start | bytes 2359304 | tf_op jit(solution)/shard_map/ppermute | solution.py:318
  80.5 15.2 %copy-start.10 = (pred[8]{0:T(512)(128)(4,1)S(1)}, pred[8]{0:T(512)(128)(4,1)}, u32[]{:S(2)}) copy-start(pred[8]{0:T(512)(128)(4,1)} %get-tuple-element.32) | copy-start | bytes 28
  80.5 15.2 %copy-start.12 = (s32[8]{0:T(128)S(1)}, s32[8]{0:T(128)}, u32[]{:S(2)}) copy-start(s32[8]{0:T(128)} %get-tuple-element.36) | copy-start | bytes 100
  96.5 14.5 %copy-start = (s32[8,16]{1,0:T(8,128)S(1)}, s32[8,16]{1,0:T(8,128)}, u32[]{:S(2)}) copy-start(s32[8,16]{1,0:T(8,128)} %select_reduce_fusion.1.where_ref) | copy-start | bytes 1540
  96.5 14.5 %copy-start.1 = (s32[4,12]{1,0:T(4,128)S(1)}, s32[4,12]{1,0:T(4,128)}, u32[]{:S(2)}) copy-start(s32[4,12]{1,0:T(4,128)} %get-tuple-element.30.column_ref) | copy-start | bytes 580
  96.5 14.5 %copy-start.2 = (s32[2]{0:T(128)S(1)}, s32[2]{0:T(128)}, u32[]{:S(2)}) copy-start(s32[2]{0:T(128)} %pad_add_fusion.place_ref) | copy-start | bytes 28
  (2 other events, 4.0 us)
